TPU v7x, 32 devices: a whole 2x2x4 slice. The times are simulated.
32 devices in a mesh: groups: 2 (over x), blk: 8 (over z, y), band: 2 (over core).
Axes of the slice: x: 2, y: 2, z: 4, core: 2. Of those that a mesh axis runs over, the one named last changes fastest.
Arguments:
- weights_slab: bfloat16 [6144, 3072], P(('groups', 'blk')), parts along dimension 0, may hold values from -2 to 2, as said below
- pairs: bfloat16 [512, 8, 3072], P(('groups', 'band'), None, 'blk'), parts along dimension 0, may hold values from -40 to 40
- occupation: int32 [512], P(('groups', 'band')), parts along dimension 0, may hold values 0 or 1
Outputs:
- screened: bfloat16 [512, 8, 3072], P(('groups', 'band'), None, 'blk'), parts along dimension 0
- sigma: float32 [16, 8], P('groups'), parts along dimension 0
There are 2 independent parts, one for each index of `groups`. A program takes and returns all parts, laid end to end along the dimension named above; each array names one. Nothing has to cross between parts.
Inputs may be any that keep to these rules, and one draw needn't show every extreme that they name: weights_slab equals its transpose.
All inputs are finite; a program needn't handle non-finite values. No bound on the sum of `occupation` on one device may be relied on, other than what follows from the above.
Results may differ from a plain program's by a relative error of at most 0.0004.
Values may be sent and summed in bfloat16 or wider, within the bound.
No kernel may reach another device: no remote copies, remote signals or barrier semaphores. Data moves between devices by JAX's collectives and lax.ppermute only.
A program may use at most 128 MiB of HBM per device.

v0:
```python
import jax
import jax.numpy as jnp
from jax import lax
from jax.sharding import PartitionSpec as P


def local(weights_slab, pairs, occupation):
    nbands = pairs.shape[0]
    nstates = pairs.shape[1]
    rows = pairs.shape[2]
    flat = pairs.reshape(nbands * nstates, rows)
    wide = lax.dot_general(
        lax.all_gather(flat, "blk", axis=1, tiled=True),
        weights_slab,
        (((1,), (1,)), ((), ())),
        preferred_element_type=jnp.float32,
    )
    wide = wide.reshape(nbands, nstates, rows)
    coeff = 0.5 - occupation.astype(jnp.float32)
    weighted = pairs.astype(jnp.float32) * coeff[:, None, None]
    partial_sigma = jnp.einsum("bqg,bpg->qp", weighted, wide, precision=lax.Precision.HIGHEST)
    slab_total = rows * lax.axis_size("blk")
    sigma = lax.psum(partial_sigma, ("blk", "band")) / (16.0 * slab_total)
    return (wide.astype(jnp.bfloat16), sigma)


def solution(mesh):
    in_specs = (
        P(("groups", "blk"), None),
        P(("groups", "band"), None, "blk"),
        P(("groups", "band")),
    )
    out_specs = (P(("groups", "band"), None, "blk"), P("groups", None))
    return jax.shard_map(local, mesh=mesh, in_specs=in_specs, out_specs=out_specs, check_vma=False)
```

profile of v0, /device:TPU:0, one launch (start us, length us, event | category | flops | bytes accessed | tf_op | source)
XLA Modules:
  0.0 161.4 jit_solution(16191678144415211467)
XLA Ops:
  7.2 0.0 copy-start
  7.2 0.0 all-gather.2.cloned.1.call-start
  7.2 0.7 all-gather.2.cloned.1.call-update
  7.9 0.7 convert_subtract_fusion
  8.6 0.0 copy-start.1
  8.6 104.2 %all-gather.2.cloned.1.call-done = bf16[1024,3072]{1,0:T(8,128)(2,1)} async-done(((bf16[1024,384]{1,0:T(8,128)(2,1)}), bf16[1024,3072]{1,0:T(8,128)(2,1)}) %all-gather.2.cloned.1.call-update) | async-done | bytes 6291472 | tf_op jit(solution)/shard_map/all_gather | solution.py:13
  112.7 0.0 copy-done
  112.7 7.1 %bitcast_convert_fusion = (bf16[128,8,384]{2,1,0:T(8,128)(2,1)}, f32[1024,384]{1,0:T(8,128)S(1)}) fusion(bf16[1024,3072]{1,0:T(8,128)(2,1)} %all-gather.2.cloned.1.call-done, bf16[384,3072]{1,0:T(8,128)(2,1)S(1)} %copy-done), kind=kOutput, calls=%fused_computation.2 | convolution fusion | flops 2416312320 | bytes 11010048 | tf_op jit(solution)/shard_map/dot_general | solution.py:12
  119.8 0.0 copy-done.1
  119.8 3.6 %fusion.4 = f32[8,8]{1,0:T(8,128)S(1)} fusion(f32[1024,384]{1,0:T(8,128)S(1)} %get-tuple-element.3, bf16[128,8,384]{2,1,0:T(8,128)(2,1)S(1)} %copy-done.1, f32[128]{0:T(128)S(1)} %convert_subtract_fusion), kind=kOutput, calls=%fused_computation.5 | convolution fusion | flops 38535168 | bytes 2360064 | tf_op jit(solution)/shard_map/bqg,bpg->qp/dot_general | solution.py:21
  123.5 30.5 %psum.7 = f32[8,8]{1,0:T(8,128)S(1)} all-reduce(f32[8,8]{1,0:T(8,128)S(1)} %fusion.4), channel_id=1, replica_groups=mesh['groups'=2,'blk'=8,'band'=2] {'blk','band'}, use_global_device_ids=true, to_apply=%region_0.0 | all-reduce | flops 64 | bytes 512 | tf_op jit(solution)/shard_map/psum | solution.py:23
  154.0 0.6 broadcast_multiply_fusion
Async XLA Ops:
  7.2 105.6 %copy-start = (bf16[384,3072]{1,0:T(8,128)(2,1)S(1)}, bf16[384,3072]{1,0:T(8,128)(2,1)}, u32[]{:S(2)}) copy-start(bf16[384,3072]{1,0:T(8,128)(2,1)} %param.3) | copy-start | bytes 7077892
  7.2 105.6 %all-gather.2.cloned.1.call-start = ((), (), s32[]{:S(2)}) async-start(), calls=%async_computation | async-start | bytes 7077888 | tf_op jit(solution)/shard_map/all_gather | solution.py:13
  8.6 111.3 %copy-start.1 = (bf16[128,8,384]{2,1,0:T(8,128)(2,1)S(1)}, bf16[128,8,384]{2,1,0:T(8,128)(2,1)}, u32[]{:S(2)}) copy-start(bf16[128,8,384]{2,1,0:T(8,128)(2,1)} %param.4) | copy-start | bytes 2359300
Sparse Core Ops, SparseCore 0:
  10.1 102.6 all-gather.1
where the time goes:
time: 162 us; the launch traced here: 161 us
  waiting for transfers between devices  105 us (65%)
  blocking collectives  30.5 us (19%)
  between operations  14 us (9%)
  matrix products  10.7 us (7%)
    all_gather x1, waiting for transfers between devices, local(): lax.all_gather(flat, 'blk', axis=1, tiled=True)  104 us
    psum x1, blocking collectives, local(): sigma = lax.psum(partial_sigma, ('blk', 'band')) / (16.0 * slab_total)  30.5 us
    dot_general x1, matrix products, local(): lax.dot_general(lax.all_gather(flat, 'blk', axis=1, tiled=True), weights_...  7.09 us
    dot_general x1, matrix products, local(): jnp.einsum('bqg,bpg->qp', weighted, wide, precision=lax.Precision.HIGHEST)  3.61 us
  transfers between devices with their start and end apart: 1, of which 1 were waited for; matrix products, arithmetic and copies ran while one was open for 0% of the time, Pallas kernels for 0%

commit v1 on v0

v1 whole, which is shorter than its diff:
```python
import jax
import jax.numpy as jnp
from jax import lax
from jax.sharding import PartitionSpec as P


def ring_order(n):
    if n == 8:
        return list(range(0, n, 2)) + list(range(n - 1, 0, -2))
    return list(range(n))


def pair_sum(x, axis, n):
    k = 1
    while k < n:
        x = x + lax.ppermute(x, axis, [(i, i ^ k) for i in range(n)])
        k *= 2
    return x


def local(weights_slab, pairs, occupation):
    nbands, nstates, rows = pairs.shape
    n = lax.axis_size("blk")
    order = ring_order(n)
    ring = jnp.array(order, jnp.int32)
    place = jnp.array([order.index(i) for i in range(n)], jnp.int32)[lax.axis_index("blk")]
    forth = [(order[i], order[(i + 1) % n]) for i in range(n)]
    back = [(b, a) for a, b in forth]
    flat = pairs.reshape(nbands * nstates, rows)
    half = nbands * nstates // 2
    parts = (flat[:half], flat[half:])

    def product(block, distance):
        owner = ring[(place + distance) % n]
        w = lax.dynamic_slice(weights_slab, (0, owner * rows), (rows, rows))
        return lax.dot_general(block, w, (((1,), (1,)), ((), ())), preferred_element_type=jnp.float32)

    acc = [product(parts[0], 0), product(parts[1], 0)]
    fw, bw = list(parts), list(parts)
    for step in range(1, n // 2 + 1):
        last = step == n // 2
        for h in (0, 1):
            if not last or h == 0:
                fw[h] = lax.ppermute(fw[h], "blk", forth)
            if not last or h == 0:
                bw[1 - h] = lax.ppermute(bw[1 - h], "blk", back)
        for h in (0, 1):
            if not last or h == 0:
                acc[h] = acc[h] + product(fw[h], -step)
                acc[1 - h] = acc[1 - h] + product(bw[1 - h], step)
    wide = jnp.concatenate(acc, axis=0)
    coeff = 0.5 - occupation.astype(jnp.float32)
    weighted = (pairs.astype(jnp.float32) * coeff[:, None, None]).astype(jnp.bfloat16).reshape(nbands * nstates, rows)
    rounded = lax.reduce_precision(wide, 8, 7)
    high = rounded.astype(jnp.bfloat16)
    low = (wide - rounded).astype(jnp.bfloat16)
    tile = 256
    gram = jnp.zeros((tile, tile), jnp.float32)
    for t in range(nbands * nstates // tile):
        s = slice(t * tile, (t + 1) * tile)
        for part in (high, low):
            gram = gram + lax.dot_general(weighted[s], part[s], (((1,), (1,)), ((), ())), preferred_element_type=jnp.float32)
    band = jnp.arange(tile) // nstates
    gram = jnp.where(band[:, None] == band[None, :], gram, 0.0)
    pick = (jnp.arange(tile)[:, None] % nstates == jnp.arange(nstates)[None, :]).astype(jnp.float32)
    folded = jnp.dot(gram, pick, precision=lax.Precision.HIGHEST)
    partial_sigma = jnp.dot(pick.T, folded, precision=lax.Precision.HIGHEST)
    sigma = pair_sum(pair_sum(partial_sigma, "band", lax.axis_size("band")), "blk", n) / (16.0 * rows * n)
    return (wide.astype(jnp.bfloat16).reshape(nbands, nstates, rows), sigma)


def solution(mesh):
    in_specs = (
        P(("groups", "blk"), None),
        P(("groups", "band"), None, "blk"),
        P(("groups", "band")),
    )
    out_specs = (P(("groups", "band"), None, "blk"), P("groups", None))
    return jax.shard_map(local, mesh=mesh, in_specs=in_specs, out_specs=out_specs, check_vma=False)
```

time: 162 us -> 91.7 us (0.57)
  waiting for transfers between devices: 105 us -> 32.8 us
  blocking collectives: 30.5 us -> 0 us
  starting transfers between devices: 0.04 us -> 20 us
  local copies, waits for them, and re-layouts: 0.01 us -> 7.48 us
  matrix products: 10.7 us -> 14.9 us
    all_gather x1 -> x0, waiting for transfers between devices: 104 us -> none  [local(): lax.all_gather(flat, 'blk', axis=1, tiled=True)]
    ppermute x0 -> x18, waiting for transfers between devices: none -> 32.8 us  [the longest x7 19.5 us: local(): fw[h] = lax.ppermute(fw[h], 'blk', forth)]
    psum x1 -> x0, blocking collectives: 30.5 us -> none  [local(): sigma = lax.psum(partial_sigma, ('blk', 'band')) / (16.0 * slab_total)]
    ppermute x0 -> x18, starting transfers between devices: none -> 20 us  [the longest x7 9.57 us: local(): bw[1 - h] = lax.ppermute(bw[1 - h], 'blk', back)]
    dot_general x2 -> x26, matrix products: 10.7 us -> 14.9 us  [the longest x16 12.4 us: product(): lax.dot_general(block, w, (((1,), (1,)), ((), ())), preferred_element_typ...]
    dynamic_slice x0 -> x2, local copies, waits for them, and re-layouts: none -> 2.94 us  [the longest x1 1.7 us: product(): owner = ring[(place + distance) % n]]
    convert_element_type x0 -> x1, local copies, waits for them, and re-layouts: none -> 2.29 us  [local(): return (wide.astype(jnp.bfloat16).reshape(nbands, nstates, rows), sigma)]
    slice x0 -> x1, local copies, waits for them, and re-layouts: none -> 2.23 us  [local(): parts = (flat[:half], flat[half:])]
  transfers between devices with their start and end apart: 1 -> 18, of which waited for: 1 -> 9; matrix products, arithmetic and copies ran while one was open for 0% -> 20% of each run, Pallas kernels for 0% -> 0%
where the time goes in v1:
time: 91.7 us; the launch traced here: 91.2 us
  waiting for transfers between devices  32.8 us (36%)
  starting transfers between devices  20 us (22%)
  matrix products  14.9 us (16%)
  between operations  13.9 us (15%)
  local copies, waits for them, and re-layouts  7.48 us (8%)
  other arithmetic  2.1 us (2%)
    ppermute x7, waiting for transfers between devices, local(): fw[h] = lax.ppermute(fw[h], 'blk', forth)  19.5 us
    dot_general x16, matrix products, product(): lax.dot_general(block, w, (((1,), (1,)), ((), ())), preferred_element_typ...  12.4 us
    ppermute x7, starting transfers between devices, local(): bw[1 - h] = lax.ppermute(bw[1 - h], 'blk', back)  9.57 us
    ppermute x7, waiting for transfers between devices, local(): bw[1 - h] = lax.ppermute(bw[1 - h], 'blk', back)  7.57 us
    ppermute x4, waiting for transfers between devices, pair_sum(): x = x + lax.ppermute(x, axis, [(i, i ^ k) for i in range(n)])  5.68 us
    ppermute x7, starting transfers between devices, local(): fw[h] = lax.ppermute(fw[h], 'blk', forth)  5.6 us
    ppermute x4, starting transfers between devices, pair_sum(): x = x + lax.ppermute(x, axis, [(i, i ^ k) for i in range(n)])  4.87 us
    convert_element_type x1, local copies, waits for them, and re-layouts, local(): return (wide.astype(jnp.bfloat16).reshape(nbands, nstates, rows), sigma)  2.29 us
  transfers between devices with their start and end apart: 18, of which 9 were waited for; matrix products, arithmetic and copies ran while one was open for 20% of the time, Pallas kernels for 0%

profile of v1, /device:TPU:0, one launch (start us, length us, event | category | flops | bytes accessed | tf_op | source)
XLA Modules:
  0.0 91.2 jit_solution(4704778338354827255)
XLA Ops:
  0.7 2.2 %slice_bitcast_fusion.1 = (bf16[512,384]{1,0:T(8,128)(2,1)}, bf16[512,384]{1,0:T(8,128)(2,1)}) fusion(bf16[128,8,384]{2,1,0:T(8,128)(2,1)} %param.6), kind=kLoop, calls=%fused_computation.31 | loop fusion | bytes 1572864 | tf_op jit(solution)/shard_map/slice | solution.py:31
  2.9 3.0 %collective-permute-start = (bf16[512,384]{1,0:T(8,128)(2,1)}, bf16[512,384]{1,0:T(8,128)(2,1)}, u32[]{:S(2)}, u32[]{:S(2)}) collective-permute-start(bf16[512,384]{1,0:T(8,128)(2,1)} %get-tuple-element.6), channel_id=1, source_target_pairs={{0,4},{4,8},{8,12},{12,14},{14,10},{10,6},{6,2},{2,0},{1,5},{5,9},... | collective-permute-start | bytes 1179656 | tf_op jit(solution)/shard_map/ppermute | solution.py:44
  5.9 2.0 %collective-permute-start.7 = (bf16[512,384]{1,0:T(8,128)(2,1)}, bf16[512,384]{1,0:T(8,128)(2,1)S(1)}, u32[]{:S(2)}, u32[]{:S(2)}) collective-permute-start(bf16[512,384]{1,0:T(8,128)(2,1)} %get-tuple-element.7), channel_id=1, source_target_pairs={{4,0},{8,4},{12,8},{14,12},{10,14},{6,10},{2,6},{0,2},{5,1},{9,5},... | collective-permute-start | bytes 1179656 | tf_op jit(solution)/shard_map/ppermute | solution.py:46
  16.5 1.7 %fusion.61 = (s32[1]{0:T(128)}, s32[1]{0:T(128)}, s32[1]{0:T(128)}, s32[1]{0:T(128)}, s32[1]{0:T(128)}, /*index=5*/s32[1]{0:T(128)}, s32[1]{0:T(128)}, s32[1]{0:T(128)}, s32[1]{0:T(128)}) fusion(s32[8]{0:T(128)} %constant.129.clone, s32[]{:T(128)S(6)} %select_n.177, s32[]{:T(128)S(6)} %select_n.174, s32[]{:T(128)S(6)} %select_n.171, s32[]{:T(128)S(6)} %select_n.168, ...), kind=kLoop, calls=%fused_computation.96 | loop fusion | bytes 108 | tf_op jit(solution)/shard_map/dynamic_slice | solution.py:34
  18.9 2.3 %fusion.29 = f32[384,512]{1,0:T(8,128)} fusion(bf16[384,3072]{1,0:T(8,128)(2,1)S(1)} %copy-done, s32[]{:T(128)S(6)} %select_n.157, bf16[128,8,384]{2,1,0:T(8,128)(2,1)} %param.6), kind=kOutput, calls=%fused_computation.52 | convolution fusion | flops 150994944 | bytes 1474564 | tf_op jit(solution)/shard_map/dot_general | solution.py:36
  27.7 2.0 %collective-permute-start.3 = (bf16[512,384]{1,0:T(8,128)(2,1)}, bf16[512,384]{1,0:T(8,128)(2,1)S(1)}, u32[]{:S(2)}, u32[]{:S(2)}) collective-permute-start(bf16[512,384]{1,0:T(8,128)(2,1)} %collective-permute-done.1), channel_id=1, source_target_pairs={{4,0},{8,4},{12,8},{14,12},{10,14},{6,10},{2,6},{0,2},{5,1},{9,5},... | collective-permute-start | bytes 1179656 | tf_op jit(solution)/shard_map/ppermute | solution.py:46
  29.9 2.0 %collective-permute-start.10 = (bf16[512,384]{1,0:T(8,128)(2,1)}, bf16[512,384]{1,0:T(8,128)(2,1)S(1)}, u32[]{:S(2)}, u32[]{:S(2)}) collective-permute-start(bf16[512,384]{1,0:T(8,128)(2,1)} %collective-permute-done.8), channel_id=1, source_target_pairs={{0,4},{4,8},{8,12},{12,14},{14,10},{10,6},{6,2},{2,0},{1,5},{5,9},... | collective-permute-start | bytes 1179656 | tf_op jit(solution)/shard_map/ppermute | solution.py:44
  31.9 1.7 %convolution_add_fusion.9 = f32[384,512]{1,0:T(8,128)S(1)} fusion(f32[384,512]{1,0:T(8,128)} %fusion.29, bf16[512,384]{1,0:T(8,128)(2,1)} %collective-permute-done, bf16[384,3072]{1,0:T(8,128)(2,1)S(1)} %copy-done, s32[]{:T(128)S(6)} %select_n.160), kind=kOutput, calls=%fused_computation.16 | convolution fusion | flops 151191552 | bytes 2260996 | tf_op jit(solution)/shard_map/dot_general | solution.py:36
  33.6 1.4 %convolution_add_fusion.8 = f32[384,512]{1,0:T(8,128)S(1)} fusion(f32[384,512]{1,0:T(8,128)S(1)} %convolution_add_fusion.9, bf16[512,384]{1,0:T(8,128)(2,1)} %collective-permute-done.1, bf16[384,3072]{1,0:T(8,128)(2,1)S(1)} %copy-done, s32[]{:T(128)S(6)} %select_n.163), kind=kOutput, calls=%fused_computation.15 | convolution fusion | flops 151191552 | bytes 2260996 | tf_op jit(solution)/shard_map/dot_general | solution.py:36
  35.4 1.4 %convolution_add_fusion.3 = f32[384,512]{1,0:T(8,128)S(1)} fusion(f32[384,512]{1,0:T(8,128)S(1)} %convolution_add_fusion.4, bf16[512,384]{1,0:T(8,128)(2,1)} %collective-permute-done.8, bf16[384,3072]{1,0:T(8,128)(2,1)S(1)} %copy-done, s32[]{:T(128)S(6)} %select_n.160), kind=kOutput, calls=%fused_computation.9 | convolution fusion | flops 151191552 | bytes 2260996 | tf_op jit(solution)/shard_map/dot_general | solution.py:36
  36.8 3.3 %collective-permute-done.3 = bf16[512,384]{1,0:T(8,128)(2,1)S(1)} collective-permute-done((bf16[512,384]{1,0:T(8,128)(2,1)}, bf16[512,384]{1,0:T(8,128)(2,1)S(1)}, u32[]{:S(2)}, u32[]{:S(2)}) %collective-permute-start.3) | collective-permute-done | bytes 393248 | tf_op jit(solution)/shard_map/ppermute | solution.py:46
  40.0 1.9 %collective-permute-start.5 = (bf16[512,384]{1,0:T(8,128)(2,1)S(1)}, bf16[512,384]{1,0:T(8,128)(2,1)S(1)}, u32[]{:S(2)}, u32[]{:S(2)}) collective-permute-start(bf16[512,384]{1,0:T(8,128)(2,1)S(1)} %collective-permute-done.3), channel_id=1, source_target_pairs={{4,0},{8,4},{12,8},{14,12},{10,14},{6,10},{2,6},{0,2},{5,1},{9,5},... | collective-permute-start | bytes 1179656 | tf_op jit(solution)/shard_map/ppermute | solution.py:46
  42.1 8.3 %collective-permute-done.10 = bf16[512,384]{1,0:T(8,128)(2,1)S(1)} collective-permute-done((bf16[512,384]{1,0:T(8,128)(2,1)}, bf16[512,384]{1,0:T(8,128)(2,1)S(1)}, u32[]{:S(2)}, u32[]{:S(2)}) %collective-permute-start.10) | collective-permute-done | bytes 393248 | tf_op jit(solution)/shard_map/ppermute | solution.py:44
  51.0 1.9 %collective-permute-start.11 = (bf16[512,384]{1,0:T(8,128)(2,1)S(1)}, bf16[512,384]{1,0:T(8,128)(2,1)S(1)}, u32[]{:S(2)}, u32[]{:S(2)}) collective-permute-start(bf16[512,384]{1,0:T(8,128)(2,1)S(1)} %collective-permute-done.9), channel_id=1, source_target_pairs={{4,0},{8,4},{12,8},{14,12},{10,14},{6,10},{2,6},{0,2},{5,1},{9,5},... | collective-permute-start | bytes 1179656 | tf_op jit(solution)/shard_map/ppermute | solution.py:46
  54.1 4.7 %collective-permute-done.4 = bf16[512,384]{1,0:T(8,128)(2,1)S(1)} collective-permute-done((bf16[512,384]{1,0:T(8,128)(2,1)S(1)}, bf16[512,384]{1,0:T(8,128)(2,1)S(1)}, u32[]{:S(2)}, u32[]{:S(2)}) %collective-permute-start.4) | collective-permute-done | bytes 393248 | tf_op jit(solution)/shard_map/ppermute | solution.py:44
  59.0 4.3 %collective-permute-done.11 = bf16[512,384]{1,0:T(8,128)(2,1)S(1)} collective-permute-done((bf16[512,384]{1,0:T(8,128)(2,1)S(1)}, bf16[512,384]{1,0:T(8,128)(2,1)S(1)}, u32[]{:S(2)}, u32[]{:S(2)}) %collective-permute-start.11) | collective-permute-done | bytes 393248 | tf_op jit(solution)/shard_map/ppermute | solution.py:46
  63.3 1.7 %collective-permute-start.13 = (bf16[512,384]{1,0:T(8,128)(2,1)S(1)}, bf16[512,384]{1,0:T(8,128)(2,1)S(1)}, u32[]{:S(2)}, u32[]{:S(2)}) collective-permute-start(bf16[512,384]{1,0:T(8,128)(2,1)S(1)} %collective-permute-done.11), channel_id=1, source_target_pairs={{4,0},{8,4},{12,8},{14,12},{10,14},{6,10},{2,6},{0,2},{5,1},{9,5},... | collective-permute-start | bytes 1179656 | tf_op jit(solution)/shard_map/ppermute | solution.py:46
  65.8 1.5 %collective-permute-done.12 = bf16[512,384]{1,0:T(8,128)(2,1)S(1)} collective-permute-done((bf16[512,384]{1,0:T(8,128)(2,1)S(1)}, bf16[512,384]{1,0:T(8,128)(2,1)S(1)}, u32[]{:S(2)}, u32[]{:S(2)}) %collective-permute-start.12) | collective-permute-done | bytes 393248 | tf_op jit(solution)/shard_map/ppermute | solution.py:44
  68.1 5.0 %collective-permute-done.6 = bf16[512,384]{1,0:T(8,128)(2,1)S(1)} collective-permute-done((bf16[512,384]{1,0:T(8,128)(2,1)S(1)}, bf16[512,384]{1,0:T(8,128)(2,1)S(1)}, u32[]{:S(2)}, u32[]{:S(2)}) %collective-permute-start.6) | collective-permute-done | bytes 393248 | tf_op jit(solution)/shard_map/ppermute | solution.py:44
  78.0 1.6 %collective-permute-start.15 = (f32[8,8]{1,0:T(8,128)S(1)}, f32[8,8]{1,0:T(8,128)S(1)}, u32[]{:S(2)}, u32[]{:S(2)}) collective-permute-start(f32[8,8]{1,0:T(8,128)S(1)} %add.305), channel_id=1, source_target_pairs={{0,2},{2,0},{4,6},{6,4},{8,10},{10,8},{12,14},{14,12},{1,3},{3,1},... | collective-permute-start | bytes 776 | tf_op jit(solution)/shard_map/ppermute | solution.py:16
  79.5 2.0 %collective-permute-done.15 = f32[8,8]{1,0:T(8,128)S(1)} collective-permute-done((f32[8,8]{1,0:T(8,128)S(1)}, f32[8,8]{1,0:T(8,128)S(1)}, u32[]{:S(2)}, u32[]{:S(2)}) %collective-permute-start.15) | collective-permute-done | bytes 288 | tf_op jit(solution)/shard_map/ppermute | solution.py:16
  82.7 2.5 %collective-permute-done.16 = f32[8,8]{1,0:T(8,128)S(1)} collective-permute-done((f32[8,8]{1,0:T(8,128)S(1)}, f32[8,8]{1,0:T(8,128)S(1)}, u32[]{:S(2)}, u32[]{:S(2)}) %collective-permute-start.16) | collective-permute-done | bytes 288 | tf_op jit(solution)/shard_map/ppermute | solution.py:16
  85.2 2.2 %collective-permute-start.17 = (f32[8,8]{1,0:T(8,128)S(1)}, f32[8,8]{1,0:T(8,128)S(1)}, u32[]{:S(2)}, u32[]{:S(2)}) collective-permute-start(f32[8,8]{1,0:T(8,128)S(1)} %add.307), channel_id=1, source_target_pairs={{0,8},{2,10},{4,12},{6,14},{8,0},{10,2},{12,4},{14,6},{1,9},{3,11}... | collective-permute-start | bytes 776 | tf_op jit(solution)/shard_map/ppermute | solution.py:16
  88.3 2.3 %copy.8 = bf16[1024,384]{1,0:T(8,128)(2,1)} copy(bf16[1024,384]{0,1:T(8,128)(2,1)} %fusion.8) | data formatting | bytes 1572864 | tf_op jit(solution)/shard_map/convert_element_type | solution.py:69
  (59 shorter events, 14.6 us)
Async XLA Ops:
  0.6 18.2 %copy-start = (bf16[384,3072]{1,0:T(8,128)(2,1)S(1)}, bf16[384,3072]{1,0:T(8,128)(2,1)}, u32[]{:S(2)}) copy-start(bf16[384,3072]{1,0:T(8,128)(2,1)} %param.5) | copy-start | bytes 7077892
  0.6 20.5 %copy-start.1 = (bf16[128,8,384]{2,1,0:T(8,128)(2,1)S(1)}, bf16[128,8,384]{2,1,0:T(8,128)(2,1)}, u32[]{:S(2)}) copy-start(bf16[128,8,384]{2,1,0:T(8,128)(2,1)} %param.6) | copy-start | bytes 2359300
  0.7 21.8 %copy-start.3 = (s32[128]{0:T(128)S(1)}, s32[128]{0:T(128)}, u32[]{:S(2)}) copy-start(s32[128]{0:T(128)} %param.7) | copy-start | bytes 1540
  2.9 26.8 %collective-permute-start = (bf16[512,384]{1,0:T(8,128)(2,1)}, bf16[512,384]{1,0:T(8,128)(2,1)}, u32[]{:S(2)}, u32[]{:S(2)}) collective-permute-start(bf16[512,384]{1,0:T(8,128)(2,1)} %get-tuple-element.6), channel_id=1, source_target_pairs={{0,4},{4,8},{8,12},{12,14},{14,10},{10,6},{6,2},{2,0},{1,5},{5,9},... | collective-permute-start | bytes 1179656 | tf_op jit(solution)/shard_map/ppermute | solution.py:44
  5.9 21.8 %collective-permute-start.1 = (bf16[512,384]{1,0:T(8,128)(2,1)}, bf16[512,384]{1,0:T(8,128)(2,1)}, u32[]{:S(2)}, u32[]{:S(2)}) collective-permute-start(bf16[512,384]{1,0:T(8,128)(2,1)} %get-tuple-element.6), channel_id=1, source_target_pairs={{4,0},{8,4},{12,8},{14,12},{10,14},{6,10},{2,6},{0,2},{5,1},{9,5},... | collective-permute-start | bytes 1179656 | tf_op jit(solution)/shard_map/ppermute | solution.py:46
  5.9 25.9 %collective-permute-start.7 = (bf16[512,384]{1,0:T(8,128)(2,1)}, bf16[512,384]{1,0:T(8,128)(2,1)S(1)}, u32[]{:S(2)}, u32[]{:S(2)}) collective-permute-start(bf16[512,384]{1,0:T(8,128)(2,1)} %get-tuple-element.7), channel_id=1, source_target_pairs={{4,0},{8,4},{12,8},{14,12},{10,14},{6,10},{2,6},{0,2},{5,1},{9,5},... | collective-permute-start | bytes 1179656 | tf_op jit(solution)/shard_map/ppermute | solution.py:46
  7.9 22.0 %collective-permute-start.8 = (bf16[512,384]{1,0:T(8,128)(2,1)}, bf16[512,384]{1,0:T(8,128)(2,1)}, u32[]{:S(2)}, u32[]{:S(2)}) collective-permute-start(bf16[512,384]{1,0:T(8,128)(2,1)} %get-tuple-element.7), channel_id=1, source_target_pairs={{0,4},{4,8},{8,12},{12,14},{14,10},{10,6},{6,2},{2,0},{1,5},{5,9},... | collective-permute-start | bytes 1179656 | tf_op jit(solution)/shard_map/ppermute | solution.py:44
  27.7 7.3 %copy-start.2 = (f32[384,512]{1,0:T(8,128)S(1)}, f32[384,512]{1,0:T(8,128)}, u32[]{:S(2)}) copy-start(f32[384,512]{1,0:T(8,128)} %fusion.27) | copy-start | bytes 2359300
  27.7 12.3 %collective-permute-start.3 = (bf16[512,384]{1,0:T(8,128)(2,1)}, bf16[512,384]{1,0:T(8,128)(2,1)S(1)}, u32[]{:S(2)}, u32[]{:S(2)}) collective-permute-start(bf16[512,384]{1,0:T(8,128)(2,1)} %collective-permute-done.1), channel_id=1, source_target_pairs={{4,0},{8,4},{12,8},{14,12},{10,14},{6,10},{2,6},{0,2},{5,1},{9,5},... | collective-permute-start | bytes 1179656 | tf_op jit(solution)/shard_map/ppermute | solution.py:46
  29.7 12.3 %collective-permute-start.2 = (bf16[512,384]{1,0:T(8,128)(2,1)}, bf16[512,384]{1,0:T(8,128)(2,1)S(1)}, u32[]{:S(2)}, u32[]{:S(2)}) collective-permute-start(bf16[512,384]{1,0:T(8,128)(2,1)} %collective-permute-done), channel_id=1, source_target_pairs={{0,4},{4,8},{8,12},{12,14},{14,10},{10,6},{6,2},{2,0},{1,5},{5,9},... | collective-permute-start | bytes 1179656 | tf_op jit(solution)/shard_map/ppermute | solution.py:44
  29.9 20.6 %collective-permute-start.10 = (bf16[512,384]{1,0:T(8,128)(2,1)}, bf16[512,384]{1,0:T(8,128)(2,1)S(1)}, u32[]{:S(2)}, u32[]{:S(2)}) collective-permute-start(bf16[512,384]{1,0:T(8,128)(2,1)} %collective-permute-done.8), channel_id=1, source_target_pairs={{0,4},{4,8},{8,12},{12,14},{14,10},{10,6},{6,2},{2,0},{1,5},{5,9},... | collective-permute-start | bytes 1179656 | tf_op jit(solution)/shard_map/ppermute | solution.py:44
  31.8 19.1 %collective-permute-start.9 = (bf16[512,384]{1,0:T(8,128)(2,1)S(1)}, bf16[512,384]{1,0:T(8,128)(2,1)S(1)}, u32[]{:S(2)}, u32[]{:S(2)}) collective-permute-start(bf16[512,384]{1,0:T(8,128)(2,1)S(1)} %collective-permute-done.7), channel_id=1, source_target_pairs={{4,0},{8,4},{12,8},{14,12},{10,14},{6,10},{2,6},{0,2},{5,1},{9,5},... | collective-permute-start | bytes 1179656 | tf_op jit(solution)/shard_map/ppermute | solution.py:46
  40.0 24.9 %collective-permute-start.5 = (bf16[512,384]{1,0:T(8,128)(2,1)S(1)}, bf16[512,384]{1,0:T(8,128)(2,1)S(1)}, u32[]{:S(2)}, u32[]{:S(2)}) collective-permute-start(bf16[512,384]{1,0:T(8,128)(2,1)S(1)} %collective-permute-done.3), channel_id=1, source_target_pairs={{4,0},{8,4},{12,8},{14,12},{10,14},{6,10},{2,6},{0,2},{5,1},{9,5},... | collective-permute-start | bytes 1179656 | tf_op jit(solution)/shard_map/ppermute | solution.py:46
  42.0 16.9 %collective-permute-start.4 = (bf16[512,384]{1,0:T(8,128)(2,1)S(1)}, bf16[512,384]{1,0:T(8,128)(2,1)S(1)}, u32[]{:S(2)}, u32[]{:S(2)}) collective-permute-start(bf16[512,384]{1,0:T(8,128)(2,1)S(1)} %collective-permute-done.2), channel_id=1, source_target_pairs={{0,4},{4,8},{8,12},{12,14},{14,10},{10,6},{6,2},{2,0},{1,5},{5,9},... | collective-permute-start | bytes 1179656 | tf_op jit(solution)/shard_map/ppermute | solution.py:44
  50.4 16.9 %collective-permute-start.12 = (bf16[512,384]{1,0:T(8,128)(2,1)S(1)}, bf16[512,384]{1,0:T(8,128)(2,1)S(1)}, u32[]{:S(2)}, u32[]{:S(2)}) collective-permute-start(bf16[512,384]{1,0:T(8,128)(2,1)S(1)} %collective-permute-done.10), channel_id=1, source_target_pairs={{0,4},{4,8},{8,12},{12,14},{14,10},{10,6},{6,2},{2,0},{1,5},{5,9},... | collective-permute-start | bytes 1179656 | tf_op jit(solution)/shard_map/ppermute | solution.py:44
  51.0 12.3 %collective-permute-start.11 = (bf16[512,384]{1,0:T(8,128)(2,1)S(1)}, bf16[512,384]{1,0:T(8,128)(2,1)S(1)}, u32[]{:S(2)}, u32[]{:S(2)}) collective-permute-start(bf16[512,384]{1,0:T(8,128)(2,1)S(1)} %collective-permute-done.9), channel_id=1, source_target_pairs={{4,0},{8,4},{12,8},{14,12},{10,14},{6,10},{2,6},{0,2},{5,1},{9,5},... | collective-permute-start | bytes 1179656 | tf_op jit(solution)/shard_map/ppermute | solution.py:46
  58.8 14.3 %collective-permute-start.6 = (bf16[512,384]{1,0:T(8,128)(2,1)S(1)}, bf16[512,384]{1,0:T(8,128)(2,1)S(1)}, u32[]{:S(2)}, u32[]{:S(2)}) collective-permute-start(bf16[512,384]{1,0:T(8,128)(2,1)S(1)} %collective-permute-done.4), channel_id=1, source_target_pairs={{0,4},{4,8},{8,12},{12,14},{14,10},{10,6},{6,2},{2,0},{1,5},{5,9},... | collective-permute-start | bytes 1179656 | tf_op jit(solution)/shard_map/ppermute | solution.py:44
  63.3 10.2 %collective-permute-start.13 = (bf16[512,384]{1,0:T(8,128)(2,1)S(1)}, bf16[512,384]{1,0:T(8,128)(2,1)S(1)}, u32[]{:S(2)}, u32[]{:S(2)}) collective-permute-start(bf16[512,384]{1,0:T(8,128)(2,1)S(1)} %collective-permute-done.11), channel_id=1, source_target_pairs={{4,0},{8,4},{12,8},{14,12},{10,14},{6,10},{2,6},{0,2},{5,1},{9,5},... | collective-permute-start | bytes 1179656 | tf_op jit(solution)/shard_map/ppermute | solution.py:46
  76.8 1.2 %collective-permute-start.14 = (f32[8,8]{1,0:T(8,128)S(1)}, f32[8,8]{1,0:T(8,128)S(1)}, u32[]{:S(2)}, u32[]{:S(2)}) collective-permute-start(f32[8,8]{1,0:T(8,128)S(1)} %fusion.40), channel_id=1, source_target_pairs={{0,1},{1,0},{2,3},{3,2},{4,5},{5,4},{6,7},{7,6},{8,9},{9,8},{10,11... | collective-permute-start | bytes 776 | tf_op jit(solution)/shard_map/ppermute | solution.py:16
  78.0 3.6 %collective-permute-start.15 = (f32[8,8]{1,0:T(8,128)S(1)}, f32[8,8]{1,0:T(8,128)S(1)}, u32[]{:S(2)}, u32[]{:S(2)}) collective-permute-start(f32[8,8]{1,0:T(8,128)S(1)} %add.305), channel_id=1, source_target_pairs={{0,2},{2,0},{4,6},{6,4},{8,10},{10,8},{12,14},{14,12},{1,3},{3,1},... | collective-permute-start | bytes 776 | tf_op jit(solution)/shard_map/ppermute | solution.py:16
  81.6 3.6 %collective-permute-start.16 = (f32[8,8]{1,0:T(8,128)S(1)}, f32[8,8]{1,0:T(8,128)S(1)}, u32[]{:S(2)}, u32[]{:S(2)}) collective-permute-start(f32[8,8]{1,0:T(8,128)S(1)} %add.306), channel_id=1, source_target_pairs={{0,4},{2,6},{4,0},{6,2},{8,12},{10,14},{12,8},{14,10},{1,5},{3,7},... | collective-permute-start | bytes 776 | tf_op jit(solution)/shard_map/ppermute | solution.py:16
  85.2 5.4 %collective-permute-start.17 = (f32[8,8]{1,0:T(8,128)S(1)}, f32[8,8]{1,0:T(8,128)S(1)}, u32[]{:S(2)}, u32[]{:S(2)}) collective-permute-start(f32[8,8]{1,0:T(8,128)S(1)} %add.307), channel_id=1, source_target_pairs={{0,8},{2,10},{4,12},{6,14},{8,0},{10,2},{12,4},{14,6},{1,9},{3,11}... | collective-permute-start | bytes 776 | tf_op jit(solution)/shard_map/ppermute | solution.py:16

commit v2 on v0

v2 whole, which is shorter than its diff:
```python
import jax
import jax.numpy as jnp
from jax import lax
from jax.sharding import PartitionSpec as P

BEFORE = 0
BESIDE = 2
HOPS = [[1, 2, 3], [4]]


def ring_order(n):
    if n == 8:
        return list(range(0, n, 2)) + list(range(n - 1, 0, -2))
    return list(range(n))


def block_starts(n, depth):
    me = lax.axis_index("blk")
    if n != 8:
        return [(me + ahead) % n * depth for ahead in range(n)]
    place = jnp.where(me % 2 == 0, me // 2, n - 1 - me // 2)
    there = [(place + ahead) % n for ahead in range(n)]
    return [jnp.where(t < n // 2, 2 * t, 2 * (n - t) - 1) * depth for t in there]


def times(left, right):
    return lax.dot_general(left, right, (((1,), (1,)), ((), ())), preferred_element_type=jnp.float32)


def gram_of(weighted, halves, tile):
    gram = jnp.zeros((tile, tile), jnp.float32)
    row = 0
    for wide in halves:
        rounded = lax.reduce_precision(wide, 8, 7)
        parts = rounded.astype(jnp.bfloat16), (wide - rounded).astype(jnp.bfloat16)
        for t in range(0, wide.shape[0], tile):
            for part in parts:
                gram = gram + times(weighted[row : row + tile], part[t : t + tile])
            row += tile
    return gram


def band_sums(gram, nstates):
    tile = gram.shape[0]
    band = jnp.arange(tile) // nstates
    gram = jnp.where(band[:, None] == band[None, :], gram, 0.0)
    pick = (jnp.arange(tile)[:, None] % nstates == jnp.arange(nstates)[None, :]).astype(jnp.float32)
    folded = jnp.dot(gram, pick, precision=lax.Precision.HIGHEST)
    return jnp.dot(pick.T, folded, precision=lax.Precision.HIGHEST)


def local(weights_slab, pairs, occupation):
    nbands, nstates, depth = pairs.shape
    rows = nbands * nstates
    n = lax.axis_size("blk")
    half = n // 2
    order = ring_order(n)
    forth = [(order[i], order[(i + 1) % n]) for i in range(n)]
    back = [(b, a) for a, b in forth]
    starts = block_starts(n, depth)
    flat = pairs.reshape(rows, depth)
    upper, lower = slice(0, rows // 2), slice(rows // 2, rows)
    together = lax.optimization_barrier

    def product(block, distance):
        return times(block, lax.dynamic_slice(weights_slab, (0, starts[distance % n]), (depth, depth)))

    def move(pair, ways):
        return [lax.ppermute(block, "blk", way) for block, way in zip(pair, ways)]

    came_forth, came_back = move([flat, flat], (forth, back))
    own = [product(flat[upper], 0), product(flat[lower], 0)]
    coeff = 0.5 - occupation.astype(jnp.float32)
    weighted = (pairs.astype(jnp.float32) * coeff[:, None, None]).astype(jnp.bfloat16).reshape(rows, depth)
    came_forth, came_back, own, weighted = together((came_forth, came_back, own, weighted))

    block, late = [came_forth[upper], came_back[lower]], [came_back[upper], came_forth[lower]]
    near = [0.5 * own[0] + product(block[0], -1), 0.5 * own[1] + product(block[1], 1)]
    rest = [0.5 * own[0] + product(late[0], 1), 0.5 * own[1] + product(late[1], -1)]
    for step in range(2, half):
        block = move(block, (forth, back))
        if step > 3:
            late = move(late, (back, forth))
        block, late, near, rest = together((block, late, near, rest))
        near = [near[0] + product(block[0], -step), near[1] + product(block[1], step)]
        if step > 3:
            rest = [rest[0] + product(late[0], step - 2), rest[1] + product(late[1], 2 - step)]

    hops = [("band", [1])] + [("blk", k) for k in HOPS] + [("blk", [1 << k]) for k in range(3, n.bit_length() - 1)]

    def exchange(share, count):
        for _ in range(count):
            axis, offsets = hops.pop(0)
            size = lax.axis_size(axis)
            share = sum([lax.ppermute(share, axis, [(i, i ^ k) for i in range(size)]) for k in offsets], share)
        return share

    far = move(block, (forth, back))
    late = move(late, (back, forth))
    gram = gram_of(weighted, near, rows // 4)
    rest = [near[h] + rest[h] for h in (0, 1)]
    far = [product(far[h], half) for h in (0, 1)]
    share = band_sums(gram + gram_of(weighted, [0.5 * f for f in far], rows // 4), nstates)
    rest = [rest[h] + far[h] for h in (0, 1)]
    share = exchange(share, BEFORE)
    late, share, rest = together((late, share, rest))
    rest = [rest[0] + product(late[0], half - 2), rest[1] + product(late[1], 2 - half)]
    late = move(late, (back, forth))
    share = exchange(share, BESIDE)
    late, share, rest = together((late, share, rest))
    rest = [rest[0] + product(late[0], half - 1), rest[1] + product(late[1], 1 - half)]
    share = exchange(share, len(hops))
    sigma = (share + share.T) / (16.0 * depth * n)
    wide = jnp.concatenate(rest, axis=0)
    return (wide.astype(jnp.bfloat16).reshape(nbands, nstates, depth), sigma)


def solution(mesh):
    in_specs = (
        P(("groups", "blk"), None),
        P(("groups", "band"), None, "blk"),
        P(("groups", "band")),
    )
    out_specs = (P(("groups", "band"), None, "blk"), P("groups", None))
    return jax.shard_map(local, mesh=mesh, in_specs=in_specs, out_specs=out_specs, check_vma=False)
```

time: 162 us -> 83 us (0.51)
  waiting for transfers between devices: 105 us -> 43.3 us
  blocking collectives: 30.5 us -> 0 us
  starting transfers between devices: 0.04 us -> 18.5 us
  between operations: 14 us -> 1 us
  matrix products: 10.7 us -> 14.8 us
  local copies, waits for them, and re-layouts: 0.01 us -> 2.52 us
    all_gather x1 -> x0, waiting for transfers between devices: 104 us -> none  [local(): lax.all_gather(flat, 'blk', axis=1, tiled=True)]
    ppermute x0 -> x17, waiting for transfers between devices: none -> 43.3 us  [the longest x12 36 us: move(): return [lax.ppermute(block, 'blk', way) for block, way in zip(pair, ways)]]
    psum x1 -> x0, blocking collectives: 30.5 us -> none  [local(): sigma = lax.psum(partial_sigma, ('blk', 'band')) / (16.0 * slab_total)]
    ppermute x0 -> x17, starting transfers between devices: none -> 18.5 us  [the longest x12 13.3 us: move(): return [lax.ppermute(block, 'blk', way) for block, way in zip(pair, ways)]]
    dot_general x2 -> x34, matrix products: 10.7 us -> 14.8 us  [the longest x32 14.2 us: times(): lax.dot_general(left, right, (((1,), (1,)), ((), ())), preferred_element_...]
  transfers between devices with their start and end apart: 1 -> 17, of which waited for: 1 -> 12; matrix products, arithmetic and copies ran while one was open for 0% -> 19% of each run, Pallas kernels for 0% -> 0%
where the time goes in v2:
time: 83 us; the launch traced here: 82.7 us
  waiting for transfers between devices  43.3 us (52%)
  starting transfers between devices  18.5 us (22%)
  matrix products  14.8 us (18%)
  other arithmetic  2.54 us (3%)
  local copies, waits for them, and re-layouts  2.52 us (3%)
  between operations  1 us (1%)
    ppermute x12, waiting for transfers between devices, move(): return [lax.ppermute(block, 'blk', way) for block, way in zip(pair, ways)]  36 us
    dot_general x32, matrix products, times(): lax.dot_general(left, right, (((1,), (1,)), ((), ())), preferred_element_...  14.2 us
    ppermute x12, starting transfers between devices, move(): return [lax.ppermute(block, 'blk', way) for block, way in zip(pair, ways)]  13.3 us
    ppermute x5, waiting for transfers between devices, exchange(): lax.ppermute(share, axis, [(i, i ^ k) for i in range(size)])  7.32 us
    ppermute x5, starting transfers between devices, exchange(): lax.ppermute(share, axis, [(i, i ^ k) for i in range(size)])  5.16 us
  transfers between devices with their start and end apart: 17, of which 12 were waited for; matrix products, arithmetic and copies ran while one was open for 19% of the time, Pallas kernels for 0%

profile of v2, /device:TPU:0, one launch (start us, length us, event | category | flops | bytes accessed | tf_op | source)
XLA Modules:
  0.0 82.7 jit_solution(17866303361818183954)
XLA Ops:
  0.6 3.1 %collective-permute-start = (bf16[1024,384]{1,0:T(8,128)(2,1)}, bf16[1024,384]{1,0:T(8,128)(2,1)S(1)}, u32[]{:S(2)}, u32[]{:S(2)}) collective-permute-start(bf16[1024,384]{1,0:T(8,128)(2,1)} %bitcast.30), channel_id=1, source_target_pairs={{0,4},{4,8},{8,12},{12,14},{14,10},{10,6},{6,2},{2,0},{1,5},{5,9},... | collective-permute-start | bytes 2359304 | tf_op jit(solution)/shard_map/ppermute | solution.py:69
  4.4 1.5 %convolution_bitcast_fusion = f32[512,384]{0,1:T(8,128)S(1)} fusion(bf16[128,8,384]{2,1,0:T(8,128)(2,1)} %param.4, bf16[384,3072]{1,0:T(8,128)(2,1)S(1)} %copy-done, s32[]{:T(128)S(6)} %select_n.138), kind=kOutput, calls=%fused_computation.5 | convolution fusion | flops 150994944 | bytes 1474564 | tf_op jit(solution)/shard_map/dot_general | solution.py:27
  5.9 1.4 %convolution_bitcast_fusion.1 = f32[512,384]{0,1:T(8,128)S(1)} fusion(bf16[128,8,384]{2,1,0:T(8,128)(2,1)} %param.4, bf16[384,3072]{1,0:T(8,128)(2,1)S(1)} %copy-done, s32[]{:T(128)S(6)} %select_n.138), kind=kOutput, calls=%fused_computation.6 | convolution fusion | flops 150994944 | bytes 1474564 | tf_op jit(solution)/shard_map/dot_general | solution.py:27
  7.5 13.9 %collective-permute-done = bf16[1024,384]{1,0:T(8,128)(2,1)S(1)} collective-permute-done((bf16[1024,384]{1,0:T(8,128)(2,1)}, bf16[1024,384]{1,0:T(8,128)(2,1)S(1)}, u32[]{:S(2)}, u32[]{:S(2)}) %collective-permute-start) | collective-permute-done | bytes 786464 | tf_op jit(solution)/shard_map/ppermute | solution.py:69
  21.4 1.6 %collective-permute-done.1 = bf16[1024,384]{1,0:T(8,128)(2,1)} collective-permute-done((bf16[1024,384]{1,0:T(8,128)(2,1)}, bf16[1024,384]{1,0:T(8,128)(2,1)}, u32[]{:S(2)}, u32[]{:S(2)}) %collective-permute-start.1) | collective-permute-done | bytes 786464 | tf_op jit(solution)/shard_map/ppermute | solution.py:69
  23.1 1.2 %fusion.98 = (bf16[512,384]{1,0:T(8,128)(2,1)S(1)}, bf16[512,384]{1,0:T(8,128)(2,1)S(1)}) fusion(bf16[1024,384]{1,0:T(8,128)(2,1)} %collective-permute-done.1), kind=kLoop, calls=%fused_computation.141 | loop fusion | bytes 1572864 | tf_op jit(solution)/shard_map/slice | solution.py:77
  24.7 1.4 %convolution_add_fusion.2 = f32[512,384]{0,1:T(8,128)S(1)} fusion(f32[512,384]{0,1:T(8,128)S(1)} %convolution_bitcast_fusion, bf16[384,3072]{1,0:T(8,128)(2,1)S(1)} %copy-done, s32[]{:T(128)S(6)} %select_n.144, bf16[1024,384]{1,0:T(8,128)(2,1)} %collective-permute-done.1), kind=kOutput, calls=%fused_computation.3 | convolution fusion | flops 151388160 | bytes 2260996 | tf_op jit(solution)/shard_map/dot_general | solution.py:27
  26.1 1.6 %collective-permute-start.2 = (bf16[512,384]{1,0:T(8,128)(2,1)S(1)}, bf16[512,384]{1,0:T(8,128)(2,1)S(1)}, u32[]{:S(2)}, u32[]{:S(2)}) collective-permute-start(bf16[512,384]{1,0:T(8,128)(2,1)S(1)} %get-tuple-element.77), channel_id=1, source_target_pairs={{0,4},{4,8},{8,12},{12,14},{14,10},{10,6},{6,2},{2,0},{1,5},{5,9},... | collective-permute-start | bytes 1179656 | tf_op jit(solution)/shard_map/ppermute | solution.py:69
  28.2 1.4 %convolution_add_fusion.1 = f32[512,384]{0,1:T(8,128)S(1)} fusion(f32[512,384]{0,1:T(8,128)S(1)} %convolution_bitcast_fusion.1, bf16[384,3072]{1,0:T(8,128)(2,1)S(1)} %copy-done, s32[]{:T(128)S(6)} %select_n.144, bf16[1024,384]{1,0:T(8,128)(2,1)} %collective-permute-done.1), kind=kOutput, calls=%fused_computation.2 | convolution fusion | flops 151388160 | bytes 2260996 | tf_op jit(solution)/shard_map/dot_general | solution.py:27
  30.0 5.8 %collective-permute-done.2 = bf16[512,384]{1,0:T(8,128)(2,1)S(1)} collective-permute-done((bf16[512,384]{1,0:T(8,128)(2,1)S(1)}, bf16[512,384]{1,0:T(8,128)(2,1)S(1)}, u32[]{:S(2)}, u32[]{:S(2)}) %collective-permute-start.2) | collective-permute-done | bytes 393248 | tf_op jit(solution)/shard_map/ppermute | solution.py:69
  35.9 1.3 %collective-permute-done.3 = bf16[512,384]{1,0:T(8,128)(2,1)S(1)} collective-permute-done((bf16[512,384]{1,0:T(8,128)(2,1)S(1)}, bf16[512,384]{1,0:T(8,128)(2,1)S(1)}, u32[]{:S(2)}, u32[]{:S(2)}) %collective-permute-start.3) | collective-permute-done | bytes 393248 | tf_op jit(solution)/shard_map/ppermute | solution.py:69
  37.2 1.6 %collective-permute-start.4 = (bf16[512,384]{1,0:T(8,128)(2,1)S(1)}, bf16[512,384]{1,0:T(8,128)(2,1)S(1)}, u32[]{:S(2)}, u32[]{:S(2)}) collective-permute-start(bf16[512,384]{1,0:T(8,128)(2,1)S(1)} %collective-permute-done.2), channel_id=1, source_target_pairs={{0,4},{4,8},{8,12},{12,14},{14,10},{10,6},{6,2},{2,0},{1,5},{5,9},... | collective-permute-start | bytes 1179656 | tf_op jit(solution)/shard_map/ppermute | solution.py:69
  40.3 5.3 %collective-permute-done.4 = bf16[512,384]{1,0:T(8,128)(2,1)S(1)} collective-permute-done((bf16[512,384]{1,0:T(8,128)(2,1)S(1)}, bf16[512,384]{1,0:T(8,128)(2,1)S(1)}, u32[]{:S(2)}, u32[]{:S(2)}) %collective-permute-start.4) | collective-permute-done | bytes 393248 | tf_op jit(solution)/shard_map/ppermute | solution.py:69
  45.6 1.3 %collective-permute-done.5 = bf16[512,384]{1,0:T(8,128)(2,1)S(1)} collective-permute-done((bf16[512,384]{1,0:T(8,128)(2,1)S(1)}, bf16[512,384]{1,0:T(8,128)(2,1)S(1)}, u32[]{:S(2)}, u32[]{:S(2)}) %collective-permute-start.5) | collective-permute-done | bytes 393248 | tf_op jit(solution)/shard_map/ppermute | solution.py:69
  46.9 2.0 %collective-permute-start.8 = (bf16[512,384]{1,0:T(8,128)(2,1)S(1)}, bf16[512,384]{1,0:T(8,128)(2,1)S(1)}, u32[]{:S(2)}, u32[]{:S(2)}) collective-permute-start(bf16[512,384]{1,0:T(8,128)(2,1)S(1)} %collective-permute-done.4), channel_id=1, source_target_pairs={{0,4},{4,8},{8,12},{12,14},{14,10},{10,6},{6,2},{2,0},{1,5},{5,9},... | collective-permute-start | bytes 1179656 | tf_op jit(solution)/shard_map/ppermute | solution.py:69
  49.4 1.6 %collective-permute-start.7 = (bf16[512,384]{1,0:T(8,128)(2,1)S(1)}, bf16[512,384]{1,0:T(8,128)(2,1)S(1)}, u32[]{:S(2)}, u32[]{:S(2)}) collective-permute-start(bf16[512,384]{1,0:T(8,128)(2,1)S(1)} %get-tuple-element.46), channel_id=1, source_target_pairs={{0,4},{4,8},{8,12},{12,14},{14,10},{10,6},{6,2},{2,0},{1,5},{5,9},... | collective-permute-start | bytes 1179656 | tf_op jit(solution)/shard_map/ppermute | solution.py:69
  51.8 6.6 %collective-permute-done.8 = bf16[512,384]{1,0:T(8,128)(2,1)S(1)} collective-permute-done((bf16[512,384]{1,0:T(8,128)(2,1)S(1)}, bf16[512,384]{1,0:T(8,128)(2,1)S(1)}, u32[]{:S(2)}, u32[]{:S(2)}) %collective-permute-start.8) | collective-permute-done | bytes 393248 | tf_op jit(solution)/shard_map/ppermute | solution.py:69
  64.3 1.5 %collective-permute-start.11 = (bf16[512,384]{1,0:T(8,128)(2,1)S(1)}, bf16[512,384]{1,0:T(8,128)(2,1)S(1)}, u32[]{:S(2)}, u32[]{:S(2)}) collective-permute-start(bf16[512,384]{1,0:T(8,128)(2,1)S(1)} %collective-permute-done.7), channel_id=1, source_target_pairs={{0,4},{4,8},{8,12},{12,14},{14,10},{10,6},{6,2},{2,0},{1,5},{5,9},... | collective-permute-start | bytes 1179656 | tf_op jit(solution)/shard_map/ppermute | solution.py:69
  67.5 0.9 %collective-permute-start.14 = (f32[8,8]{1,0:T(8,128)S(1)}, f32[8,8]{1,0:T(8,128)S(1)}, u32[]{:S(2)}, u32[]{:S(2)}) collective-permute-start(f32[8,8]{1,0:T(8,128)S(1)} %add.275), channel_id=1, source_target_pairs={{0,4},{2,6},{4,0},{6,2},{8,12},{10,14},{12,8},{14,10},{1,5},{3,7},... | collective-permute-start | bytes 776 | tf_op jit(solution)/shard_map/ppermute | solution.py:95
  68.4 2.0 %collective-permute-start.15 = (f32[8,8]{1,0:T(8,128)S(1)}, f32[8,8]{1,0:T(8,128)S(1)}, u32[]{:S(2)}, u32[]{:S(2)}) collective-permute-start(f32[8,8]{1,0:T(8,128)S(1)} %add.275), channel_id=1, source_target_pairs={{0,6},{2,4},{4,2},{6,0},{8,14},{10,12},{12,10},{14,8},{1,7},{3,5},... | collective-permute-start | bytes 776 | tf_op jit(solution)/shard_map/ppermute | solution.py:95
  70.7 4.8 %collective-permute-done.13 = f32[8,8]{1,0:T(8,128)S(1)} collective-permute-done((f32[8,8]{1,0:T(8,128)S(1)}, f32[8,8]{1,0:T(8,128)S(1)}, u32[]{:S(2)}, u32[]{:S(2)}) %collective-permute-start.13) | collective-permute-done | bytes 288 | tf_op jit(solution)/shard_map/ppermute | solution.py:95
  75.5 1.9 %collective-permute-done.14 = f32[8,8]{1,0:T(8,128)S(1)} collective-permute-done((f32[8,8]{1,0:T(8,128)S(1)}, f32[8,8]{1,0:T(8,128)S(1)}, u32[]{:S(2)}, u32[]{:S(2)}) %collective-permute-start.14) | collective-permute-done | bytes 288 | tf_op jit(solution)/shard_map/ppermute | solution.py:95
  77.4 1.7 %collective-permute-start.16 = (f32[8,8]{1,0:T(8,128)S(1)}, f32[8,8]{1,0:T(8,128)S(1)}, u32[]{:S(2)}, u32[]{:S(2)}) collective-permute-start(f32[8,8]{1,0:T(8,128)S(1)} %add_add_fusion.2), channel_id=1, source_target_pairs={{0,8},{2,10},{4,12},{6,14},{8,0},{10,2},{12,4},{14,6},{1,9},{3,11}... | collective-permute-start | bytes 776 | tf_op jit(solution)/shard_map/ppermute | solution.py:95
  80.4 1.2 %copy.39 = bf16[1024,384]{1,0:T(8,128)(2,1)} copy(bf16[1024,384]{0,1:T(8,128)(2,1)S(1)} %pad_maximum_fusion) | data formatting | bytes 1572864 | tf_op jit(solution)/shard_map/concatenate | solution.py:114
  (66 shorter events, 15.1 us)
Async XLA Ops:
  0.6 3.8 %copy-start = (bf16[384,3072]{1,0:T(8,128)(2,1)S(1)}, bf16[384,3072]{1,0:T(8,128)(2,1)}, u32[]{:S(2)}) copy-start(bf16[384,3072]{1,0:T(8,128)(2,1)} %param.3) | copy-start | bytes 7077892
  0.6 20.8 %collective-permute-start = (bf16[1024,384]{1,0:T(8,128)(2,1)}, bf16[1024,384]{1,0:T(8,128)(2,1)S(1)}, u32[]{:S(2)}, u32[]{:S(2)}) collective-permute-start(bf16[1024,384]{1,0:T(8,128)(2,1)} %bitcast.30), channel_id=1, source_target_pairs={{0,4},{4,8},{8,12},{12,14},{14,10},{10,6},{6,2},{2,0},{1,5},{5,9},... | collective-permute-start | bytes 2359304 | tf_op jit(solution)/shard_map/ppermute | solution.py:69
  3.7 19.3 %collective-permute-start.1 = (bf16[1024,384]{1,0:T(8,128)(2,1)}, bf16[1024,384]{1,0:T(8,128)(2,1)}, u32[]{:S(2)}, u32[]{:S(2)}) collective-permute-start(bf16[1024,384]{1,0:T(8,128)(2,1)} %bitcast.31), channel_id=1, source_target_pairs={{4,0},{8,4},{12,8},{14,12},{10,14},{6,10},{2,6},{0,2},{5,1},{9,5},... | collective-permute-start | bytes 2359304 | tf_op jit(solution)/shard_map/ppermute | solution.py:69
  4.4 2.9 %copy-start.1 = (bf16[128,8,384]{2,1,0:T(8,128)(2,1)S(1)}, bf16[128,8,384]{2,1,0:T(8,128)(2,1)}, u32[]{:S(2)}) copy-start(bf16[128,8,384]{2,1,0:T(8,128)(2,1)} %param.4) | copy-start | bytes 2359300
  26.1 9.7 %collective-permute-start.2 = (bf16[512,384]{1,0:T(8,128)(2,1)S(1)}, bf16[512,384]{1,0:T(8,128)(2,1)S(1)}, u32[]{:S(2)}, u32[]{:S(2)}) collective-permute-start(bf16[512,384]{1,0:T(8,128)(2,1)S(1)} %get-tuple-element.77), channel_id=1, source_target_pairs={{0,4},{4,8},{8,12},{12,14},{14,10},{10,6},{6,2},{2,0},{1,5},{5,9},... | collective-permute-start | bytes 1179656 | tf_op jit(solution)/shard_map/ppermute | solution.py:69
  27.8 9.4 %collective-permute-start.3 = (bf16[512,384]{1,0:T(8,128)(2,1)S(1)}, bf16[512,384]{1,0:T(8,128)(2,1)S(1)}, u32[]{:S(2)}, u32[]{:S(2)}) collective-permute-start(bf16[512,384]{1,0:T(8,128)(2,1)S(1)} %get-tuple-element.79), channel_id=1, source_target_pairs={{4,0},{8,4},{12,8},{14,12},{10,14},{6,10},{2,6},{0,2},{5,1},{9,5},... | collective-permute-start | bytes 1179656 | tf_op jit(solution)/shard_map/ppermute | solution.py:69
  37.2 8.5 %collective-permute-start.4 = (bf16[512,384]{1,0:T(8,128)(2,1)S(1)}, bf16[512,384]{1,0:T(8,128)(2,1)S(1)}, u32[]{:S(2)}, u32[]{:S(2)}) collective-permute-start(bf16[512,384]{1,0:T(8,128)(2,1)S(1)} %collective-permute-done.2), channel_id=1, source_target_pairs={{0,4},{4,8},{8,12},{12,14},{14,10},{10,6},{6,2},{2,0},{1,5},{5,9},... | collective-permute-start | bytes 1179656 | tf_op jit(solution)/shard_map/ppermute | solution.py:69
  38.7 8.2 %collective-permute-start.5 = (bf16[512,384]{1,0:T(8,128)(2,1)S(1)}, bf16[512,384]{1,0:T(8,128)(2,1)S(1)}, u32[]{:S(2)}, u32[]{:S(2)}) collective-permute-start(bf16[512,384]{1,0:T(8,128)(2,1)S(1)} %collective-permute-done.3), channel_id=1, source_target_pairs={{4,0},{8,4},{12,8},{14,12},{10,14},{6,10},{2,6},{0,2},{5,1},{9,5},... | collective-permute-start | bytes 1179656 | tf_op jit(solution)/shard_map/ppermute | solution.py:69
  46.9 11.5 %collective-permute-start.8 = (bf16[512,384]{1,0:T(8,128)(2,1)S(1)}, bf16[512,384]{1,0:T(8,128)(2,1)S(1)}, u32[]{:S(2)}, u32[]{:S(2)}) collective-permute-start(bf16[512,384]{1,0:T(8,128)(2,1)S(1)} %collective-permute-done.4), channel_id=1, source_target_pairs={{0,4},{4,8},{8,12},{12,14},{14,10},{10,6},{6,2},{2,0},{1,5},{5,9},... | collective-permute-start | bytes 1179656 | tf_op jit(solution)/shard_map/ppermute | solution.py:69
  48.9 10.9 %collective-permute-start.9 = (bf16[512,384]{1,0:T(8,128)(2,1)S(1)}, bf16[512,384]{1,0:T(8,128)(2,1)S(1)}, u32[]{:S(2)}, u32[]{:S(2)}) collective-permute-start(bf16[512,384]{1,0:T(8,128)(2,1)S(1)} %collective-permute-done.5), channel_id=1, source_target_pairs={{4,0},{8,4},{12,8},{14,12},{10,14},{6,10},{2,6},{0,2},{5,1},{9,5},... | collective-permute-start | bytes 1179656 | tf_op jit(solution)/shard_map/ppermute | solution.py:69
  48.9 14.9 %collective-permute-start.6 = (bf16[512,384]{1,0:T(8,128)(2,1)S(1)}, bf16[512,384]{1,0:T(8,128)(2,1)S(1)}, u32[]{:S(2)}, u32[]{:S(2)}) collective-permute-start(bf16[512,384]{1,0:T(8,128)(2,1)S(1)} %get-tuple-element.45), channel_id=1, source_target_pairs={{4,0},{8,4},{12,8},{14,12},{10,14},{6,10},{2,6},{0,2},{5,1},{9,5},... | collective-permute-start | bytes 1179656 | tf_op jit(solution)/shard_map/ppermute | solution.py:69
  49.4 14.5 %collective-permute-start.7 = (bf16[512,384]{1,0:T(8,128)(2,1)S(1)}, bf16[512,384]{1,0:T(8,128)(2,1)S(1)}, u32[]{:S(2)}, u32[]{:S(2)}) collective-permute-start(bf16[512,384]{1,0:T(8,128)(2,1)S(1)} %get-tuple-element.46), channel_id=1, source_target_pairs={{0,4},{4,8},{8,12},{12,14},{14,10},{10,6},{6,2},{2,0},{1,5},{5,9},... | collective-permute-start | bytes 1179656 | tf_op jit(solution)/shard_map/ppermute | solution.py:69
  64.3 13.2 %collective-permute-start.11 = (bf16[512,384]{1,0:T(8,128)(2,1)S(1)}, bf16[512,384]{1,0:T(8,128)(2,1)S(1)}, u32[]{:S(2)}, u32[]{:S(2)}) collective-permute-start(bf16[512,384]{1,0:T(8,128)(2,1)S(1)} %collective-permute-done.7), channel_id=1, source_target_pairs={{0,4},{4,8},{8,12},{12,14},{14,10},{10,6},{6,2},{2,0},{1,5},{5,9},... | collective-permute-start | bytes 1179656 | tf_op jit(solution)/shard_map/ppermute | solution.py:69
  65.8 1.2 %collective-permute-start.12 = (f32[8,8]{1,0:T(8,128)S(1)}, f32[8,8]{1,0:T(8,128)S(1)}, u32[]{:S(2)}, u32[]{:S(2)}) collective-permute-start(f32[8,8]{1,0:T(8,128)S(1)} %fusion.55), channel_id=1, source_target_pairs={{0,1},{1,0},{2,3},{3,2},{4,5},{5,4},{6,7},{7,6},{8,9},{9,8},{10,11... | collective-permute-start | bytes 776 | tf_op jit(solution)/shard_map/ppermute | solution.py:95
  65.8 11.7 %collective-permute-start.10 = (bf16[512,384]{1,0:T(8,128)(2,1)S(1)}, bf16[512,384]{1,0:T(8,128)(2,1)S(1)}, u32[]{:S(2)}, u32[]{:S(2)}) collective-permute-start(bf16[512,384]{1,0:T(8,128)(2,1)S(1)} %collective-permute-done.6), channel_id=1, source_target_pairs={{4,0},{8,4},{12,8},{14,12},{10,14},{6,10},{2,6},{0,2},{5,1},{9,5},... | collective-permute-start | bytes 1179656 | tf_op jit(solution)/shard_map/ppermute | solution.py:69
  66.9 8.6 %collective-permute-start.13 = (f32[8,8]{1,0:T(8,128)S(1)}, f32[8,8]{1,0:T(8,128)S(1)}, u32[]{:S(2)}, u32[]{:S(2)}) collective-permute-start(f32[8,8]{1,0:T(8,128)S(1)} %add.275), channel_id=1, source_target_pairs={{0,2},{2,0},{4,6},{6,4},{8,10},{10,8},{12,14},{14,12},{1,3},{3,1},... | collective-permute-start | bytes 776 | tf_op jit(solution)/shard_map/ppermute | solution.py:95
  67.5 9.9 %collective-permute-start.14 = (f32[8,8]{1,0:T(8,128)S(1)}, f32[8,8]{1,0:T(8,128)S(1)}, u32[]{:S(2)}, u32[]{:S(2)}) collective-permute-start(f32[8,8]{1,0:T(8,128)S(1)} %add.275), channel_id=1, source_target_pairs={{0,4},{2,6},{4,0},{6,2},{8,12},{10,14},{12,8},{14,10},{1,5},{3,7},... | collective-permute-start | bytes 776 | tf_op jit(solution)/shard_map/ppermute | solution.py:95
  68.4 9.0 %collective-permute-start.15 = (f32[8,8]{1,0:T(8,128)S(1)}, f32[8,8]{1,0:T(8,128)S(1)}, u32[]{:S(2)}, u32[]{:S(2)}) collective-permute-start(f32[8,8]{1,0:T(8,128)S(1)} %add.275), channel_id=1, source_target_pairs={{0,6},{2,4},{4,2},{6,0},{8,14},{10,12},{12,10},{14,8},{1,7},{3,5},... | collective-permute-start | bytes 776 | tf_op jit(solution)/shard_map/ppermute | solution.py:95
  77.4 4.6 %collective-permute-start.16 = (f32[8,8]{1,0:T(8,128)S(1)}, f32[8,8]{1,0:T(8,128)S(1)}, u32[]{:S(2)}, u32[]{:S(2)}) collective-permute-start(f32[8,8]{1,0:T(8,128)S(1)} %add_add_fusion.2), channel_id=1, source_target_pairs={{0,8},{2,10},{4,12},{6,14},{8,0},{10,2},{12,4},{14,6},{1,9},{3,11}... | collective-permute-start | bytes 776 | tf_op jit(solution)/shard_map/ppermute | solution.py:95

commit v3 on v2

--- a/solution.py
+++ b/solution.py
@@ -2,10 +2,6 @@
 import jax.numpy as jnp
 from jax import lax
 from jax.sharding import PartitionSpec as P
-
-BEFORE = 0
-BESIDE = 2
-HOPS = [[1, 2, 3], [4]]
 
 
 def ring_order(n):
@@ -27,17 +23,14 @@
     return lax.dot_general(left, right, (((1,), (1,)), ((), ())), preferred_element_type=jnp.float32)
 
 
-def gram_of(weighted, halves, tile):
-    gram = jnp.zeros((tile, tile), jnp.float32)
-    row = 0
-    for wide in halves:
-        rounded = lax.reduce_precision(wide, 8, 7)
-        parts = rounded.astype(jnp.bfloat16), (wide - rounded).astype(jnp.bfloat16)
-        for t in range(0, wide.shape[0], tile):
-            for part in parts:
-                gram = gram + times(weighted[row : row + tile], part[t : t + tile])
-            row += tile
-    return gram
+def two_terms(x):
+    rounded = lax.reduce_precision(x, 8, 7)
+    return rounded.astype(jnp.bfloat16), (x - rounded).astype(jnp.bfloat16)
+
+
+def gram_of(left, right, tile):
+    cuts = [slice(t, t + tile) for t in range(0, left.shape[0], tile)]
+    return sum(times(left[s], right[s]) for s in cuts)
 
 
 def band_sums(gram, nstates):
@@ -72,7 +65,10 @@
     own = [product(flat[upper], 0), product(flat[lower], 0)]
     coeff = 0.5 - occupation.astype(jnp.float32)
     weighted = (pairs.astype(jnp.float32) * coeff[:, None, None]).astype(jnp.bfloat16).reshape(rows, depth)
-    came_forth, came_back, own, weighted = together((came_forth, came_back, own, weighted))
+    opposite = lax.dynamic_slice(weights_slab, (0, starts[half]), (depth, depth))
+    across = lax.dot_general(weighted, opposite, (((1,), (0,)), ((), ())), preferred_element_type=jnp.float32)
+    across = two_terms(0.5 * across)
+    came_forth, came_back, own, weighted, across = together((came_forth, came_back, own, weighted, across))
 
     block, late = [came_forth[upper], came_back[lower]], [came_back[upper], came_forth[lower]]
     near = [0.5 * own[0] + product(block[0], -1), 0.5 * own[1] + product(block[1], 1)]
@@ -86,7 +82,8 @@
         if step > 3:
             rest = [rest[0] + product(late[0], step - 2), rest[1] + product(late[1], 2 - step)]
 
-    hops = [("band", [1])] + [("blk", k) for k in HOPS] + [("blk", [1 << k]) for k in range(3, n.bit_length() - 1)]
+    hops = [("blk", k) for k in ([1, 2, 3], [4])] + [("blk", [1 << k]) for k in range(3, n.bit_length() - 1)]
+    hops.insert(2, ("band", [1]))
 
     def exchange(share, count):
         for _ in range(count):
@@ -95,18 +92,24 @@
             share = sum([lax.ppermute(share, axis, [(i, i ^ k) for i in range(size)]) for k in offsets], share)
         return share
 
+    tile = rows // 4
     far = move(block, (forth, back))
+    gram = 0.0
+    for h, side in enumerate((upper, lower)):
+        gram = gram + sum(gram_of(weighted[side], part, tile) for part in two_terms(near[h]))
+    late, gram = together((late, gram))
     late = move(late, (back, forth))
-    gram = gram_of(weighted, near, rows // 4)
+    gram, far = together((gram, far))
+    for h, side in enumerate((upper, lower)):
+        gram = gram + sum(gram_of(part[side], far[h], tile) for part in across)
+    share = band_sums(gram, nstates)
     rest = [near[h] + rest[h] for h in (0, 1)]
     far = [product(far[h], half) for h in (0, 1)]
-    share = band_sums(gram + gram_of(weighted, [0.5 * f for f in far], rows // 4), nstates)
     rest = [rest[h] + far[h] for h in (0, 1)]
-    share = exchange(share, BEFORE)
     late, share, rest = together((late, share, rest))
     rest = [rest[0] + product(late[0], half - 2), rest[1] + product(late[1], 2 - half)]
     late = move(late, (back, forth))
-    share = exchange(share, BESIDE)
+    share = exchange(share, 2)
     late, share, rest = together((late, share, rest))
     rest = [rest[0] + product(late[0], half - 1), rest[1] + product(late[1], 1 - half)]
     share = exchange(share, len(hops))

time: 83 us -> 79.4 us (0.957)
  waiting for transfers between devices: 43.3 us -> 33 us
  matrix products: 14.8 us -> 18.5 us
  local copies, waits for them, and re-layouts: 2.52 us -> 3.64 us
  starting transfers between devices: 18.5 us -> 19.5 us
    ppermute x12, waiting for transfers between devices: 36 us -> 29.9 us  [move(): return [lax.ppermute(block, 'blk', way) for block, way in zip(pair, ways)]]
    ppermute x5, waiting for transfers between devices: 7.32 us -> 3.12 us  [exchange(): lax.ppermute(share, axis, [(i, i ^ k) for i in range(size)])]
    dot_general x32, matrix products: 14.2 us -> 17.1 us  [times(): lax.dot_general(left, right, (((1,), (1,)), ((), ())), preferred_element_...]
    reshape x1, other arithmetic: 0.2 us -> 1.34 us  [local(): (pairs.astype(jnp.float32) * coeff[:, None, None]).astype(jnp.bfloat16)]
    slice x1, local copies, waits for them, and re-layouts: 0.08 us -> 1.19 us  [local(): came_forth[lower]]
    ppermute x5, starting transfers between devices: 5.16 us -> 6.07 us  [exchange(): lax.ppermute(share, axis, [(i, i ^ k) for i in range(size)])]
  transfers between devices with their start and end apart: 17 -> 17, of which waited for: 12 -> 10; matrix products, arithmetic and copies ran while one was open for 19% -> 28% of each run, Pallas kernels for 0% -> 0%
where the time goes in v3:
time: 79.4 us; the launch traced here: 79 us
  waiting for transfers between devices  33 us (42%)
  starting transfers between devices  19.5 us (25%)
  matrix products  18.5 us (23%)
  local copies, waits for them, and re-layouts  3.64 us (5%)
  other arithmetic  3.03 us (4%)
  between operations  1.22 us (2%)
    ppermute x12, waiting for transfers between devices, move(): return [lax.ppermute(block, 'blk', way) for block, way in zip(pair, ways)]  29.9 us
    dot_general x32, matrix products, times(): lax.dot_general(left, right, (((1,), (1,)), ((), ())), preferred_element_...  17.1 us
    ppermute x12, starting transfers between devices, move(): return [lax.ppermute(block, 'blk', way) for block, way in zip(pair, ways)]  13.5 us
    ppermute x5, starting transfers between devices, exchange(): lax.ppermute(share, axis, [(i, i ^ k) for i in range(size)])  6.07 us
    ppermute x5, waiting for transfers between devices, exchange(): lax.ppermute(share, axis, [(i, i ^ k) for i in range(size)])  3.12 us
  transfers between devices with their start and end apart: 17, of which 10 were waited for; matrix products, arithmetic and copies ran while one was open for 28% of the time, Pallas kernels for 0%

profile of v3, /device:TPU:0, one launch (start us, length us, event | category | flops | bytes accessed | tf_op | source)
XLA Modules:
  0.0 79.0 jit_solution(9527320567691128709)
XLA Ops:
  0.7 3.1 %collective-permute-start = (bf16[1024,384]{1,0:T(8,128)(2,1)}, bf16[1024,384]{1,0:T(8,128)(2,1)}, u32[]{:S(2)}, u32[]{:S(2)}) collective-permute-start(bf16[1024,384]{1,0:T(8,128)(2,1)} %bitcast.30), channel_id=1, source_target_pairs={{0,4},{4,8},{8,12},{12,14},{14,10},{10,6},{6,2},{2,0},{1,5},{5,9},... | collective-permute-start | bytes 2359304 | tf_op jit(solution)/shard_map/ppermute | solution.py:62
  3.7 2.3 %convolution_bitcast_fusion.1 = f32[512,384]{0,1:T(8,128)} fusion(bf16[128,8,384]{2,1,0:T(8,128)(2,1)} %param.4, bf16[384,3072]{1,0:T(8,128)(2,1)S(1)} %copy-done, s32[]{:T(128)S(6)} %select_n.139), kind=kOutput, calls=%fused_computation.10 | convolution fusion | flops 150994944 | bytes 1474564 | tf_op jit(solution)/shard_map/dot_general | solution.py:23
  6.1 1.4 %convolution_bitcast_fusion = f32[512,384]{0,1:T(8,128)S(1)} fusion(bf16[128,8,384]{2,1,0:T(8,128)(2,1)} %param.4, bf16[384,3072]{1,0:T(8,128)(2,1)S(1)} %copy-done, s32[]{:T(128)S(6)} %select_n.139), kind=kOutput, calls=%fused_computation.9 | convolution fusion | flops 150994944 | bytes 1474564 | tf_op jit(solution)/shard_map/dot_general | solution.py:23
  7.7 1.3 %fusion.8 = bf16[1024,384]{1,0:T(8,128)(2,1)S(1)} fusion(bf16[128,8,384]{2,1,0:T(8,128)(2,1)} %param.4, f32[128]{0:T(128)S(1)} %convert_subtract_fusion), kind=kLoop, calls=%fused_computation.30 | loop fusion | flops 1179648 | bytes 1573376 | tf_op jit(solution)/shard_map/reshape | solution.py:67
  9.7 11.8 %collective-permute-done = bf16[1024,384]{1,0:T(8,128)(2,1)} collective-permute-done((bf16[1024,384]{1,0:T(8,128)(2,1)}, bf16[1024,384]{1,0:T(8,128)(2,1)}, u32[]{:S(2)}, u32[]{:S(2)}) %collective-permute-start) | collective-permute-done | bytes 786464 | tf_op jit(solution)/shard_map/ppermute | solution.py:62
  21.5 1.5 %collective-permute-done.1 = bf16[1024,384]{1,0:T(8,128)(2,1)} collective-permute-done((bf16[1024,384]{1,0:T(8,128)(2,1)}, bf16[1024,384]{1,0:T(8,128)(2,1)}, u32[]{:S(2)}, u32[]{:S(2)}) %collective-permute-start.1) | collective-permute-done | bytes 786464 | tf_op jit(solution)/shard_map/ppermute | solution.py:62
  23.0 1.2 %fusion.119 = (bf16[512,384]{1,0:T(8,128)(2,1)S(1)}, bf16[512,384]{1,0:T(8,128)(2,1)S(1)}) fusion(bf16[1024,384]{1,0:T(8,128)(2,1)} %collective-permute-done), kind=kLoop, calls=%fused_computation.151 | loop fusion | bytes 1572864 | tf_op jit(solution)/shard_map/slice | solution.py:73
  24.2 1.6 %collective-permute-start.2 = (bf16[512,384]{1,0:T(8,128)(2,1)S(1)}, bf16[512,384]{1,0:T(8,128)(2,1)S(1)}, u32[]{:S(2)}, u32[]{:S(2)}) collective-permute-start(bf16[512,384]{1,0:T(8,128)(2,1)S(1)} %get-tuple-element.89), channel_id=1, source_target_pairs={{0,4},{4,8},{8,12},{12,14},{14,10},{10,6},{6,2},{2,0},{1,5},{5,9},... | collective-permute-start | bytes 1179656 | tf_op jit(solution)/shard_map/ppermute | solution.py:62
  25.9 1.2 %fusion.120 = (bf16[512,384]{1,0:T(8,128)(2,1)S(1)}, bf16[512,384]{1,0:T(8,128)(2,1)S(1)}) fusion(bf16[1024,384]{1,0:T(8,128)(2,1)} %collective-permute-done.1), kind=kLoop, calls=%fused_computation.152 | loop fusion | bytes 1572864 | tf_op jit(solution)/shard_map/slice | solution.py:73
  27.6 1.4 %convolution_add_fusion.3 = f32[512,384]{0,1:T(8,128)S(1)} fusion(f32[512,384]{0,1:T(8,128)S(1)} %copy-done.1, bf16[384,3072]{1,0:T(8,128)(2,1)S(1)} %copy-done, s32[]{:T(128)S(6)} %select_n.145, bf16[1024,384]{1,0:T(8,128)(2,1)} %collective-permute-done), kind=kOutput, calls=%fused_computation.8 | convolution fusion | flops 151388160 | bytes 2260996 | tf_op jit(solution)/shard_map/dot_general | solution.py:23
  29.0 1.4 %convolution_add_fusion.1 = f32[512,384]{0,1:T(8,128)S(1)} fusion(f32[512,384]{0,1:T(8,128)S(1)} %copy-done.1, bf16[384,3072]{1,0:T(8,128)(2,1)S(1)} %copy-done, s32[]{:T(128)S(6)} %select_n.148, bf16[1024,384]{1,0:T(8,128)(2,1)} %collective-permute-done.1), kind=kOutput, calls=%fused_computation.6 | convolution fusion | flops 151388160 | bytes 2260996 | tf_op jit(solution)/shard_map/dot_general | solution.py:23
  30.4 1.4 %convolution_add_fusion.2 = f32[512,384]{0,1:T(8,128)S(1)} fusion(f32[512,384]{0,1:T(8,128)S(1)} %convolution_bitcast_fusion, bf16[384,3072]{1,0:T(8,128)(2,1)S(1)} %copy-done, s32[]{:T(128)S(6)} %select_n.148, bf16[1024,384]{1,0:T(8,128)(2,1)} %collective-permute-done.1), kind=kOutput, calls=%fused_computation.7 | convolution fusion | flops 151388160 | bytes 2260996 | tf_op jit(solution)/shard_map/dot_general | solution.py:23
  31.8 1.4 %convolution_add_fusion = f32[512,384]{0,1:T(8,128)S(1)} fusion(f32[512,384]{0,1:T(8,128)S(1)} %convolution_bitcast_fusion, bf16[384,3072]{1,0:T(8,128)(2,1)S(1)} %copy-done, s32[]{:T(128)S(6)} %select_n.145, bf16[1024,384]{1,0:T(8,128)(2,1)} %collective-permute-done), kind=kOutput, calls=%fused_computation.5 | convolution fusion | flops 151388160 | bytes 2260996 | tf_op jit(solution)/shard_map/dot_general | solution.py:23
  34.0 2.5 %collective-permute-done.3 = bf16[512,384]{1,0:T(8,128)(2,1)S(1)} collective-permute-done((bf16[512,384]{1,0:T(8,128)(2,1)S(1)}, bf16[512,384]{1,0:T(8,128)(2,1)S(1)}, u32[]{:S(2)}, u32[]{:S(2)}) %collective-permute-start.3) | collective-permute-done | bytes 393248 | tf_op jit(solution)/shard_map/ppermute | solution.py:62
  36.5 1.6 %collective-permute-start.4 = (bf16[512,384]{1,0:T(8,128)(2,1)S(1)}, bf16[512,384]{1,0:T(8,128)(2,1)S(1)}, u32[]{:S(2)}, u32[]{:S(2)}) collective-permute-start(bf16[512,384]{1,0:T(8,128)(2,1)S(1)} %collective-permute-done.2), channel_id=1, source_target_pairs={{0,4},{4,8},{8,12},{12,14},{14,10},{10,6},{6,2},{2,0},{1,5},{5,9},... | collective-permute-start | bytes 1179656 | tf_op jit(solution)/shard_map/ppermute | solution.py:62
  39.6 5.3 %collective-permute-done.4 = bf16[512,384]{1,0:T(8,128)(2,1)S(1)} collective-permute-done((bf16[512,384]{1,0:T(8,128)(2,1)S(1)}, bf16[512,384]{1,0:T(8,128)(2,1)S(1)}, u32[]{:S(2)}, u32[]{:S(2)}) %collective-permute-start.4) | collective-permute-done | bytes 393248 | tf_op jit(solution)/shard_map/ppermute | solution.py:62
  45.0 2.4 %collective-permute-done.5 = bf16[512,384]{1,0:T(8,128)(2,1)S(1)} collective-permute-done((bf16[512,384]{1,0:T(8,128)(2,1)S(1)}, bf16[512,384]{1,0:T(8,128)(2,1)S(1)}, u32[]{:S(2)}, u32[]{:S(2)}) %collective-permute-start.5) | collective-permute-done | bytes 393248 | tf_op jit(solution)/shard_map/ppermute | solution.py:62
  48.9 1.6 %collective-permute-start.8 = (bf16[512,384]{1,0:T(8,128)(2,1)S(1)}, bf16[512,384]{1,0:T(8,128)(2,1)S(1)}, u32[]{:S(2)}, u32[]{:S(2)}) collective-permute-start(bf16[512,384]{1,0:T(8,128)(2,1)S(1)} %collective-permute-done.4), channel_id=1, source_target_pairs={{0,4},{4,8},{8,12},{12,14},{14,10},{10,6},{6,2},{2,0},{1,5},{5,9},... | collective-permute-start | bytes 1179656 | tf_op jit(solution)/shard_map/ppermute | solution.py:62
  52.6 1.6 %collective-permute-start.7 = (bf16[512,384]{1,0:T(8,128)(2,1)S(1)}, bf16[512,384]{1,0:T(8,128)(2,1)S(1)}, u32[]{:S(2)}, u32[]{:S(2)}) collective-permute-start(bf16[512,384]{1,0:T(8,128)(2,1)S(1)} %get-tuple-element.61), channel_id=1, source_target_pairs={{0,4},{4,8},{8,12},{12,14},{14,10},{10,6},{6,2},{2,0},{1,5},{5,9},... | collective-permute-start | bytes 1179656 | tf_op jit(solution)/shard_map/ppermute | solution.py:62
  54.2 4.9 %collective-permute-done.8 = bf16[512,384]{1,0:T(8,128)(2,1)S(1)} collective-permute-done((bf16[512,384]{1,0:T(8,128)(2,1)S(1)}, bf16[512,384]{1,0:T(8,128)(2,1)S(1)}, u32[]{:S(2)}, u32[]{:S(2)}) %collective-permute-start.8) | collective-permute-done | bytes 393248 | tf_op jit(solution)/shard_map/ppermute | solution.py:62
  65.3 1.6 %collective-permute-start.12 = (f32[8,8]{1,0:T(8,128)S(1)}, f32[8,8]{1,0:T(8,128)S(1)}, u32[]{:S(2)}, u32[]{:S(2)}) collective-permute-start(f32[8,8]{1,0:T(8,128)S(1)} %fusion.91), channel_id=1, source_target_pairs={{0,2},{2,0},{4,6},{6,4},{8,10},{10,8},{12,14},{14,12},{1,3},{3,1},... | collective-permute-start | bytes 776 | tf_op jit(solution)/shard_map/ppermute | solution.py:92
  67.7 1.7 %collective-permute-start.11 = (bf16[512,384]{1,0:T(8,128)(2,1)S(1)}, bf16[512,384]{1,0:T(8,128)(2,1)S(1)}, u32[]{:S(2)}, u32[]{:S(2)}) collective-permute-start(bf16[512,384]{1,0:T(8,128)(2,1)S(1)} %collective-permute-done.7), channel_id=1, source_target_pairs={{0,4},{4,8},{8,12},{12,14},{14,10},{10,6},{6,2},{2,0},{1,5},{5,9},... | collective-permute-start | bytes 1179656 | tf_op jit(solution)/shard_map/ppermute | solution.py:62
  69.4 2.5 %collective-permute-start.15 = (f32[8,8]{1,0:T(8,128)S(1)}, f32[8,8]{1,0:T(8,128)S(1)}, u32[]{:S(2)}, u32[]{:S(2)}) collective-permute-start(f32[8,8]{1,0:T(8,128)S(1)} %add_add_fusion.2), channel_id=1, source_target_pairs={{0,8},{2,10},{4,12},{6,14},{8,0},{10,2},{12,4},{14,6},{1,9},{3,11}... | collective-permute-start | bytes 776 | tf_op jit(solution)/shard_map/ppermute | solution.py:92
  72.6 3.1 %collective-permute-done.15 = f32[8,8]{1,0:T(8,128)S(1)} collective-permute-done((f32[8,8]{1,0:T(8,128)S(1)}, f32[8,8]{1,0:T(8,128)S(1)}, u32[]{:S(2)}, u32[]{:S(2)}) %collective-permute-start.15) | collective-permute-done | bytes 288 | tf_op jit(solution)/shard_map/ppermute | solution.py:92
  (69 shorter events, 17.9 us)
Async XLA Ops:
  0.6 3.1 %copy-start = (bf16[384,3072]{1,0:T(8,128)(2,1)S(1)}, bf16[384,3072]{1,0:T(8,128)(2,1)}, u32[]{:S(2)}) copy-start(bf16[384,3072]{1,0:T(8,128)(2,1)} %param.3) | copy-start | bytes 7077892
  0.6 7.0 %copy-start.2 = (s32[128]{0:T(128)S(1)}, s32[128]{0:T(128)}, u32[]{:S(2)}) copy-start(s32[128]{0:T(128)} %param.5) | copy-start | bytes 1540
  0.7 20.9 %collective-permute-start = (bf16[1024,384]{1,0:T(8,128)(2,1)}, bf16[1024,384]{1,0:T(8,128)(2,1)}, u32[]{:S(2)}, u32[]{:S(2)}) collective-permute-start(bf16[1024,384]{1,0:T(8,128)(2,1)} %bitcast.30), channel_id=1, source_target_pairs={{0,4},{4,8},{8,12},{12,14},{14,10},{10,6},{6,2},{2,0},{1,5},{5,9},... | collective-permute-start | bytes 2359304 | tf_op jit(solution)/shard_map/ppermute | solution.py:62
  3.7 19.3 %collective-permute-start.1 = (bf16[1024,384]{1,0:T(8,128)(2,1)}, bf16[1024,384]{1,0:T(8,128)(2,1)}, u32[]{:S(2)}, u32[]{:S(2)}) collective-permute-start(bf16[1024,384]{1,0:T(8,128)(2,1)} %bitcast.31), channel_id=1, source_target_pairs={{4,0},{8,4},{12,8},{14,12},{10,14},{6,10},{2,6},{0,2},{5,1},{9,5},... | collective-permute-start | bytes 2359304 | tf_op jit(solution)/shard_map/ppermute | solution.py:62
  9.1 18.5 %copy-start.1 = (f32[512,384]{0,1:T(8,128)S(1)}, f32[512,384]{0,1:T(8,128)}, u32[]{:S(2)}) copy-start(f32[512,384]{0,1:T(8,128)} %convolution_bitcast_fusion.1) | copy-start | bytes 2359300
  24.2 9.7 %collective-permute-start.2 = (bf16[512,384]{1,0:T(8,128)(2,1)S(1)}, bf16[512,384]{1,0:T(8,128)(2,1)S(1)}, u32[]{:S(2)}, u32[]{:S(2)}) collective-permute-start(bf16[512,384]{1,0:T(8,128)(2,1)S(1)} %get-tuple-element.89), channel_id=1, source_target_pairs={{0,4},{4,8},{8,12},{12,14},{14,10},{10,6},{6,2},{2,0},{1,5},{5,9},... | collective-permute-start | bytes 1179656 | tf_op jit(solution)/shard_map/ppermute | solution.py:62
  27.1 9.4 %collective-permute-start.3 = (bf16[512,384]{1,0:T(8,128)(2,1)S(1)}, bf16[512,384]{1,0:T(8,128)(2,1)S(1)}, u32[]{:S(2)}, u32[]{:S(2)}) collective-permute-start(bf16[512,384]{1,0:T(8,128)(2,1)S(1)} %get-tuple-element.91), channel_id=1, source_target_pairs={{4,0},{8,4},{12,8},{14,12},{10,14},{6,10},{2,6},{0,2},{5,1},{9,5},... | collective-permute-start | bytes 1179656 | tf_op jit(solution)/shard_map/ppermute | solution.py:62
  36.5 8.5 %collective-permute-start.4 = (bf16[512,384]{1,0:T(8,128)(2,1)S(1)}, bf16[512,384]{1,0:T(8,128)(2,1)S(1)}, u32[]{:S(2)}, u32[]{:S(2)}) collective-permute-start(bf16[512,384]{1,0:T(8,128)(2,1)S(1)} %collective-permute-done.2), channel_id=1, source_target_pairs={{0,4},{4,8},{8,12},{12,14},{14,10},{10,6},{6,2},{2,0},{1,5},{5,9},... | collective-permute-start | bytes 1179656 | tf_op jit(solution)/shard_map/ppermute | solution.py:62
  38.1 9.3 %collective-permute-start.5 = (bf16[512,384]{1,0:T(8,128)(2,1)S(1)}, bf16[512,384]{1,0:T(8,128)(2,1)S(1)}, u32[]{:S(2)}, u32[]{:S(2)}) collective-permute-start(bf16[512,384]{1,0:T(8,128)(2,1)S(1)} %collective-permute-done.3), channel_id=1, source_target_pairs={{4,0},{8,4},{12,8},{14,12},{10,14},{6,10},{2,6},{0,2},{5,1},{9,5},... | collective-permute-start | bytes 1179656 | tf_op jit(solution)/shard_map/ppermute | solution.py:62
  47.4 11.7 %collective-permute-start.9 = (bf16[512,384]{1,0:T(8,128)(2,1)S(1)}, bf16[512,384]{1,0:T(8,128)(2,1)S(1)}, u32[]{:S(2)}, u32[]{:S(2)}) collective-permute-start(bf16[512,384]{1,0:T(8,128)(2,1)S(1)} %collective-permute-done.5), channel_id=1, source_target_pairs={{4,0},{8,4},{12,8},{14,12},{10,14},{6,10},{2,6},{0,2},{5,1},{9,5},... | collective-permute-start | bytes 1179656 | tf_op jit(solution)/shard_map/ppermute | solution.py:62
  48.9 10.2 %collective-permute-start.8 = (bf16[512,384]{1,0:T(8,128)(2,1)S(1)}, bf16[512,384]{1,0:T(8,128)(2,1)S(1)}, u32[]{:S(2)}, u32[]{:S(2)}) collective-permute-start(bf16[512,384]{1,0:T(8,128)(2,1)S(1)} %collective-permute-done.4), channel_id=1, source_target_pairs={{0,4},{4,8},{8,12},{12,14},{14,10},{10,6},{6,2},{2,0},{1,5},{5,9},... | collective-permute-start | bytes 1179656 | tf_op jit(solution)/shard_map/ppermute | solution.py:62
  52.1 11.1 %collective-permute-start.6 = (bf16[512,384]{1,0:T(8,128)(2,1)S(1)}, bf16[512,384]{1,0:T(8,128)(2,1)S(1)}, u32[]{:S(2)}, u32[]{:S(2)}) collective-permute-start(bf16[512,384]{1,0:T(8,128)(2,1)S(1)} %get-tuple-element.60), channel_id=1, source_target_pairs={{4,0},{8,4},{12,8},{14,12},{10,14},{6,10},{2,6},{0,2},{5,1},{9,5},... | collective-permute-start | bytes 1179656 | tf_op jit(solution)/shard_map/ppermute | solution.py:62
  52.6 10.7 %collective-permute-start.7 = (bf16[512,384]{1,0:T(8,128)(2,1)S(1)}, bf16[512,384]{1,0:T(8,128)(2,1)S(1)}, u32[]{:S(2)}, u32[]{:S(2)}) collective-permute-start(bf16[512,384]{1,0:T(8,128)(2,1)S(1)} %get-tuple-element.61), channel_id=1, source_target_pairs={{0,4},{4,8},{8,12},{12,14},{14,10},{10,6},{6,2},{2,0},{1,5},{5,9},... | collective-permute-start | bytes 1179656 | tf_op jit(solution)/shard_map/ppermute | solution.py:62
  63.4 6.0 %collective-permute-start.14 = (f32[8,8]{1,0:T(8,128)S(1)}, f32[8,8]{1,0:T(8,128)S(1)}, u32[]{:S(2)}, u32[]{:S(2)}) collective-permute-start(f32[8,8]{1,0:T(8,128)S(1)} %fusion.91), channel_id=1, source_target_pairs={{0,6},{2,4},{4,2},{6,0},{8,14},{10,12},{12,10},{14,8},{1,7},{3,5},... | collective-permute-start | bytes 776 | tf_op jit(solution)/shard_map/ppermute | solution.py:92
  64.4 4.9 %collective-permute-start.13 = (f32[8,8]{1,0:T(8,128)S(1)}, f32[8,8]{1,0:T(8,128)S(1)}, u32[]{:S(2)}, u32[]{:S(2)}) collective-permute-start(f32[8,8]{1,0:T(8,128)S(1)} %fusion.91), channel_id=1, source_target_pairs={{0,4},{2,6},{4,0},{6,2},{8,12},{10,14},{12,8},{14,10},{1,5},{3,7},... | collective-permute-start | bytes 776 | tf_op jit(solution)/shard_map/ppermute | solution.py:92
  65.3 4.1 %collective-permute-start.12 = (f32[8,8]{1,0:T(8,128)S(1)}, f32[8,8]{1,0:T(8,128)S(1)}, u32[]{:S(2)}, u32[]{:S(2)}) collective-permute-start(f32[8,8]{1,0:T(8,128)S(1)} %fusion.91), channel_id=1, source_target_pairs={{0,2},{2,0},{4,6},{6,4},{8,10},{10,8},{12,14},{14,12},{1,3},{3,1},... | collective-permute-start | bytes 776 | tf_op jit(solution)/shard_map/ppermute | solution.py:92
  66.9 8.8 %collective-permute-start.10 = (bf16[512,384]{1,0:T(8,128)(2,1)S(1)}, bf16[512,384]{1,0:T(8,128)(2,1)S(1)}, u32[]{:S(2)}, u32[]{:S(2)}) collective-permute-start(bf16[512,384]{1,0:T(8,128)(2,1)S(1)} %collective-permute-done.6), channel_id=1, source_target_pairs={{4,0},{8,4},{12,8},{14,12},{10,14},{6,10},{2,6},{0,2},{5,1},{9,5},... | collective-permute-start | bytes 1179656 | tf_op jit(solution)/shard_map/ppermute | solution.py:62
  67.7 8.0 %collective-permute-start.11 = (bf16[512,384]{1,0:T(8,128)(2,1)S(1)}, bf16[512,384]{1,0:T(8,128)(2,1)S(1)}, u32[]{:S(2)}, u32[]{:S(2)}) collective-permute-start(bf16[512,384]{1,0:T(8,128)(2,1)S(1)} %collective-permute-done.7), channel_id=1, source_target_pairs={{0,4},{4,8},{8,12},{12,14},{14,10},{10,6},{6,2},{2,0},{1,5},{5,9},... | collective-permute-start | bytes 1179656 | tf_op jit(solution)/shard_map/ppermute | solution.py:62
  69.4 6.3 %collective-permute-start.15 = (f32[8,8]{1,0:T(8,128)S(1)}, f32[8,8]{1,0:T(8,128)S(1)}, u32[]{:S(2)}, u32[]{:S(2)}) collective-permute-start(f32[8,8]{1,0:T(8,128)S(1)} %add_add_fusion.2), channel_id=1, source_target_pairs={{0,8},{2,10},{4,12},{6,14},{8,0},{10,2},{12,4},{14,6},{1,9},{3,11}... | collective-permute-start | bytes 776 | tf_op jit(solution)/shard_map/ppermute | solution.py:92
  76.5 1.7 %collective-permute-start.16 = (f32[8,8]{1,0:T(8,128)S(1)}, f32[8,8]{1,0:T(8,128)S(1)}, u32[]{:S(2)}, u32[]{:S(2)}) collective-permute-start(f32[8,8]{1,0:T(8,128)S(1)} %add.279), channel_id=1, source_target_pairs={{0,1},{1,0},{2,3},{3,2},{4,5},{5,4},{6,7},{7,6},{8,9},{9,8},{10,11... | collective-permute-start | bytes 776 | tf_op jit(solution)/shard_map/ppermute | solution.py:92

commit v4 on v3

--- a/solution.py
+++ b/solution.py
@@ -70,14 +70,17 @@
     across = two_terms(0.5 * across)
     came_forth, came_back, own, weighted, across = together((came_forth, came_back, own, weighted, across))
 
-    block, late = [came_forth[upper], came_back[lower]], [came_back[upper], came_forth[lower]]
+    block, came, late = [came_forth[upper], came_back[lower]], (came_back, came_forth), None
     near = [0.5 * own[0] + product(block[0], -1), 0.5 * own[1] + product(block[1], 1)]
-    rest = [0.5 * own[0] + product(late[0], 1), 0.5 * own[1] + product(late[1], -1)]
+    rest = [0.5 * o for o in own]
     for step in range(2, half):
         block = move(block, (forth, back))
         if step > 3:
             late = move(late, (back, forth))
-        block, late, near, rest = together((block, late, near, rest))
+        block, late, near, rest, came = together((block, late, near, rest, came))
+        if step == 2:
+            late = [came[0][upper], came[1][lower]]
+            rest = [rest[0] + product(late[0], 1), rest[1] + product(late[1], -1)]
         near = [near[0] + product(block[0], -step), near[1] + product(block[1], step)]
         if step > 3:
             rest = [rest[0] + product(late[0], step - 2), rest[1] + product(late[1], 2 - step)]
@@ -106,7 +109,7 @@
     rest = [near[h] + rest[h] for h in (0, 1)]
     far = [product(far[h], half) for h in (0, 1)]
     rest = [rest[h] + far[h] for h in (0, 1)]
-    late, share, rest = together((late, share, rest))
+    late, rest = together((late, rest))
     rest = [rest[0] + product(late[0], half - 2), rest[1] + product(late[1], 2 - half)]
     late = move(late, (back, forth))
     share = exchange(share, 2)

time: 79.4 us -> 78.7 us (level)
  waiting for transfers between devices: 33 us -> 30.1 us
  local copies, waits for them, and re-layouts: 3.64 us -> 5.4 us
    ppermute x12, waiting for transfers between devices: 29.9 us -> 27 us  [move(): return [lax.ppermute(block, 'blk', way) for block, way in zip(pair, ways)]]
    slice x2 -> x4, local copies, waits for them, and re-layouts: 2.39 us -> 4.14 us  [the longest x2 2.07 us: local(): late = [came[0][upper], came[1][lower]]]
  transfers between devices with their start and end apart: 17 -> 17, of which waited for: 10 -> 8; matrix products, arithmetic and copies ran while one was open for 28% -> 32% of each run, Pallas kernels for 0% -> 0%
where the time goes in v4:
time: 78.7 us; the launch traced here: 78.1 us
  waiting for transfers between devices  30.1 us (38%)
  starting transfers between devices  19.6 us (25%)
  matrix products  18.5 us (24%)
  local copies, waits for them, and re-layouts  5.4 us (7%)
  other arithmetic  3.43 us (4%)
  between operations  1.06 us (1%)
    ppermute x12, waiting for transfers between devices, move(): return [lax.ppermute(block, 'blk', way) for block, way in zip(pair, ways)]  27 us
    dot_general x32, matrix products, times(): lax.dot_general(left, right, (((1,), (1,)), ((), ())), preferred_element_...  17.1 us
    ppermute x12, starting transfers between devices, move(): return [lax.ppermute(block, 'blk', way) for block, way in zip(pair, ways)]  13.5 us
    ppermute x5, starting transfers between devices, exchange(): lax.ppermute(share, axis, [(i, i ^ k) for i in range(size)])  6.08 us
    ppermute x5, waiting for transfers between devices, exchange(): lax.ppermute(share, axis, [(i, i ^ k) for i in range(size)])  3.12 us
    slice x2, local copies, waits for them, and re-layouts, local(): late = [came[0][upper], came[1][lower]]  2.07 us
  transfers between devices with their start and end apart: 17, of which 8 were waited for; matrix products, arithmetic and copies ran while one was open for 32% of the time, Pallas kernels for 0%

profile of v4, /device:TPU:0, one launch (start us, length us, event | category | flops | bytes accessed | tf_op | source)
XLA Modules:
  0.0 78.1 jit_solution(9859452069609251877)
XLA Ops:
  0.7 3.1 %collective-permute-start = (bf16[1024,384]{1,0:T(8,128)(2,1)}, bf16[1024,384]{1,0:T(8,128)(2,1)}, u32[]{:S(2)}, u32[]{:S(2)}) collective-permute-start(bf16[1024,384]{1,0:T(8,128)(2,1)} %bitcast.30), channel_id=1, source_target_pairs={{0,4},{4,8},{8,12},{12,14},{14,10},{10,6},{6,2},{2,0},{1,5},{5,9},... | collective-permute-start | bytes 2359304 | tf_op jit(solution)/shard_map/ppermute | solution.py:62
  3.7 1.4 %convolution_bitcast_fusion.1 = f32[512,384]{0,1:T(8,128)S(1)} fusion(bf16[128,8,384]{2,1,0:T(8,128)(2,1)} %param.4, bf16[384,3072]{1,0:T(8,128)(2,1)S(1)} %copy-done, s32[]{:T(128)S(6)} %select_n.139), kind=kOutput, calls=%fused_computation.8 | convolution fusion | flops 150994944 | bytes 1474564 | tf_op jit(solution)/shard_map/dot_general | solution.py:23
  5.2 2.3 %convolution_bitcast_fusion = f32[512,384]{0,1:T(8,128)} fusion(bf16[128,8,384]{2,1,0:T(8,128)(2,1)} %param.4, bf16[384,3072]{1,0:T(8,128)(2,1)S(1)} %copy-done, s32[]{:T(128)S(6)} %select_n.139), kind=kOutput, calls=%fused_computation.7 | convolution fusion | flops 150994944 | bytes 1474564 | tf_op jit(solution)/shard_map/dot_general | solution.py:23
  7.5 1.3 %fusion.8 = bf16[1024,384]{1,0:T(8,128)(2,1)S(1)} fusion(bf16[128,8,384]{2,1,0:T(8,128)(2,1)} %param.4, f32[128]{0:T(128)S(1)} %convert_subtract_fusion), kind=kLoop, calls=%fused_computation.28 | loop fusion | flops 1179648 | bytes 1573376 | tf_op jit(solution)/shard_map/reshape | solution.py:67
  9.5 12.0 %collective-permute-done = bf16[1024,384]{1,0:T(8,128)(2,1)} collective-permute-done((bf16[1024,384]{1,0:T(8,128)(2,1)}, bf16[1024,384]{1,0:T(8,128)(2,1)}, u32[]{:S(2)}, u32[]{:S(2)}) %collective-permute-start) | collective-permute-done | bytes 786464 | tf_op jit(solution)/shard_map/ppermute | solution.py:62
  21.5 1.5 %collective-permute-done.1 = bf16[1024,384]{1,0:T(8,128)(2,1)} collective-permute-done((bf16[1024,384]{1,0:T(8,128)(2,1)}, bf16[1024,384]{1,0:T(8,128)(2,1)}, u32[]{:S(2)}, u32[]{:S(2)}) %collective-permute-start.1) | collective-permute-done | bytes 786464 | tf_op jit(solution)/shard_map/ppermute | solution.py:62
  24.1 1.6 %collective-permute-start.2 = (bf16[512,384]{1,0:T(8,128)(2,1)S(1)}, bf16[512,384]{1,0:T(8,128)(2,1)S(1)}, u32[]{:S(2)}, u32[]{:S(2)}) collective-permute-start(bf16[512,384]{1,0:T(8,128)(2,1)S(1)} %slice.128), channel_id=1, source_target_pairs={{0,4},{4,8},{8,12},{12,14},{14,10},{10,6},{6,2},{2,0},{1,5},{5,9},... | collective-permute-start | bytes 1179656 | tf_op jit(solution)/shard_map/ppermute | solution.py:62
  27.3 1.4 %convolution_add_fusion.1 = f32[512,384]{0,1:T(8,128)S(1)} fusion(bf16[384,3072]{1,0:T(8,128)(2,1)S(1)} %copy-done, s32[]{:T(128)S(6)} %select_n.145, f32[512,384]{0,1:T(8,128)S(1)} %convolution_bitcast_fusion.1, bf16[1024,384]{1,0:T(8,128)(2,1)} %collective-permute-done), kind=kOutput, calls=%fused_computation.6 | convolution fusion | flops 151388160 | bytes 2260996 | tf_op jit(solution)/shard_map/dot_general | solution.py:23
  28.7 1.4 %convolution_add_fusion = f32[512,384]{0,1:T(8,128)S(1)} fusion(bf16[384,3072]{1,0:T(8,128)(2,1)S(1)} %copy-done, s32[]{:T(128)S(6)} %select_n.148, f32[512,384]{0,1:T(8,128)S(1)} %copy-done.1, bf16[1024,384]{1,0:T(8,128)(2,1)} %collective-permute-done.1), kind=kOutput, calls=%fused_computation.5 | convolution fusion | flops 151388160 | bytes 2260996 | tf_op jit(solution)/shard_map/dot_general | solution.py:23
  30.2 3.6 %collective-permute-done.2 = bf16[512,384]{1,0:T(8,128)(2,1)S(1)} collective-permute-done((bf16[512,384]{1,0:T(8,128)(2,1)S(1)}, bf16[512,384]{1,0:T(8,128)(2,1)S(1)}, u32[]{:S(2)}, u32[]{:S(2)}) %collective-permute-start.2) | collective-permute-done | bytes 393248 | tf_op jit(solution)/shard_map/ppermute | solution.py:62
  33.8 2.4 %collective-permute-done.3 = bf16[512,384]{1,0:T(8,128)(2,1)S(1)} collective-permute-done((bf16[512,384]{1,0:T(8,128)(2,1)S(1)}, bf16[512,384]{1,0:T(8,128)(2,1)S(1)}, u32[]{:S(2)}, u32[]{:S(2)}) %collective-permute-start.3) | collective-permute-done | bytes 393248 | tf_op jit(solution)/shard_map/ppermute | solution.py:62
  36.2 1.6 %collective-permute-start.4 = (bf16[512,384]{1,0:T(8,128)(2,1)S(1)}, bf16[512,384]{1,0:T(8,128)(2,1)S(1)}, u32[]{:S(2)}, u32[]{:S(2)}) collective-permute-start(bf16[512,384]{1,0:T(8,128)(2,1)S(1)} %collective-permute-done.2), channel_id=1, source_target_pairs={{0,4},{4,8},{8,12},{12,14},{14,10},{10,6},{6,2},{2,0},{1,5},{5,9},... | collective-permute-start | bytes 1179656 | tf_op jit(solution)/shard_map/ppermute | solution.py:62
  41.4 1.4 %fusion.34 = f32[512,384]{0,1:T(8,128)S(1)} fusion(bf16[384,3072]{1,0:T(8,128)(2,1)S(1)} %copy-done, s32[]{:T(128)S(6)} %select_n.148, bf16[1024,384]{1,0:T(8,128)(2,1)} %collective-permute-done.1), kind=kOutput, calls=%fused_computation.61 | convolution fusion | flops 150994944 | bytes 1474564 | tf_op jit(solution)/shard_map/dot_general | solution.py:23
  43.0 1.4 %fusion.37 = f32[512,384]{0,1:T(8,128)S(1)} fusion(bf16[384,3072]{1,0:T(8,128)(2,1)S(1)} %copy-done, s32[]{:T(128)S(6)} %select_n.145, bf16[1024,384]{1,0:T(8,128)(2,1)} %collective-permute-done), kind=kOutput, calls=%fused_computation.64 | convolution fusion | flops 150994944 | bytes 1474564 | tf_op jit(solution)/shard_map/dot_general | solution.py:23
  44.7 2.4 %collective-permute-done.5 = bf16[512,384]{1,0:T(8,128)(2,1)S(1)} collective-permute-done((bf16[512,384]{1,0:T(8,128)(2,1)S(1)}, bf16[512,384]{1,0:T(8,128)(2,1)S(1)}, u32[]{:S(2)}, u32[]{:S(2)}) %collective-permute-start.5) | collective-permute-done | bytes 393248 | tf_op jit(solution)/shard_map/ppermute | solution.py:62
  48.6 1.6 %collective-permute-start.8 = (bf16[512,384]{1,0:T(8,128)(2,1)S(1)}, bf16[512,384]{1,0:T(8,128)(2,1)S(1)}, u32[]{:S(2)}, u32[]{:S(2)}) collective-permute-start(bf16[512,384]{1,0:T(8,128)(2,1)S(1)} %collective-permute-done.4), channel_id=1, source_target_pairs={{0,4},{4,8},{8,12},{12,14},{14,10},{10,6},{6,2},{2,0},{1,5},{5,9},... | collective-permute-start | bytes 1179656 | tf_op jit(solution)/shard_map/ppermute | solution.py:62
  52.3 1.6 %collective-permute-start.7 = (bf16[512,384]{1,0:T(8,128)(2,1)S(1)}, bf16[512,384]{1,0:T(8,128)(2,1)S(1)}, u32[]{:S(2)}, u32[]{:S(2)}) collective-permute-start(bf16[512,384]{1,0:T(8,128)(2,1)S(1)} %slice.131), channel_id=1, source_target_pairs={{0,4},{4,8},{8,12},{12,14},{14,10},{10,6},{6,2},{2,0},{1,5},{5,9},... | collective-permute-start | bytes 1179656 | tf_op jit(solution)/shard_map/ppermute | solution.py:62
  53.9 4.9 %collective-permute-done.8 = bf16[512,384]{1,0:T(8,128)(2,1)S(1)} collective-permute-done((bf16[512,384]{1,0:T(8,128)(2,1)S(1)}, bf16[512,384]{1,0:T(8,128)(2,1)S(1)}, u32[]{:S(2)}, u32[]{:S(2)}) %collective-permute-start.8) | collective-permute-done | bytes 393248 | tf_op jit(solution)/shard_map/ppermute | solution.py:62
  61.6 1.1 %collective-permute-start.14 = (f32[8,8]{1,0:T(8,128)S(1)}, f32[8,8]{1,0:T(8,128)S(1)}, u32[]{:S(2)}, u32[]{:S(2)}) collective-permute-start(f32[8,8]{1,0:T(8,128)S(1)} %fusion.93), channel_id=1, source_target_pairs={{0,6},{2,4},{4,2},{6,0},{8,14},{10,12},{12,10},{14,8},{1,7},{3,5},... | collective-permute-start | bytes 776 | tf_op jit(solution)/shard_map/ppermute | solution.py:95
  63.5 1.6 %collective-permute-start.12 = (f32[8,8]{1,0:T(8,128)S(1)}, f32[8,8]{1,0:T(8,128)S(1)}, u32[]{:S(2)}, u32[]{:S(2)}) collective-permute-start(f32[8,8]{1,0:T(8,128)S(1)} %fusion.93), channel_id=1, source_target_pairs={{0,2},{2,0},{4,6},{6,4},{8,10},{10,8},{12,14},{14,12},{1,3},{3,1},... | collective-permute-start | bytes 776 | tf_op jit(solution)/shard_map/ppermute | solution.py:95
  66.9 1.6 %collective-permute-start.11 = (bf16[512,384]{1,0:T(8,128)(2,1)S(1)}, bf16[512,384]{1,0:T(8,128)(2,1)S(1)}, u32[]{:S(2)}, u32[]{:S(2)}) collective-permute-start(bf16[512,384]{1,0:T(8,128)(2,1)S(1)} %collective-permute-done.7), channel_id=1, source_target_pairs={{0,4},{4,8},{8,12},{12,14},{14,10},{10,6},{6,2},{2,0},{1,5},{5,9},... | collective-permute-start | bytes 1179656 | tf_op jit(solution)/shard_map/ppermute | solution.py:62
  68.5 2.5 %collective-permute-start.15 = (f32[8,8]{1,0:T(8,128)S(1)}, f32[8,8]{1,0:T(8,128)S(1)}, u32[]{:S(2)}, u32[]{:S(2)}) collective-permute-start(f32[8,8]{1,0:T(8,128)S(1)} %add_add_fusion.2), channel_id=1, source_target_pairs={{0,8},{2,10},{4,12},{6,14},{8,0},{10,2},{12,4},{14,6},{1,9},{3,11}... | collective-permute-start | bytes 776 | tf_op jit(solution)/shard_map/ppermute | solution.py:95
  71.7 3.1 %collective-permute-done.15 = f32[8,8]{1,0:T(8,128)S(1)} collective-permute-done((f32[8,8]{1,0:T(8,128)S(1)}, f32[8,8]{1,0:T(8,128)S(1)}, u32[]{:S(2)}, u32[]{:S(2)}) %collective-permute-start.15) | collective-permute-done | bytes 288 | tf_op jit(solution)/shard_map/ppermute | solution.py:95
  76.2 1.2 %copy.35 = bf16[1024,384]{1,0:T(8,128)(2,1)} copy(bf16[1024,384]{0,1:T(8,128)(2,1)S(1)} %pad_maximum_fusion) | data formatting | bytes 1572864 | tf_op jit(solution)/shard_map/concatenate | solution.py:120
  (74 shorter events, 19.0 us)
Async XLA Ops:
  0.6 3.1 %copy-start = (bf16[384,3072]{1,0:T(8,128)(2,1)S(1)}, bf16[384,3072]{1,0:T(8,128)(2,1)}, u32[]{:S(2)}) copy-start(bf16[384,3072]{1,0:T(8,128)(2,1)} %param.3) | copy-start | bytes 7077892
  0.6 6.8 %copy-start.2 = (s32[128]{0:T(128)S(1)}, s32[128]{0:T(128)}, u32[]{:S(2)}) copy-start(s32[128]{0:T(128)} %param.5) | copy-start | bytes 1540
  0.7 20.9 %collective-permute-start = (bf16[1024,384]{1,0:T(8,128)(2,1)}, bf16[1024,384]{1,0:T(8,128)(2,1)}, u32[]{:S(2)}, u32[]{:S(2)}) collective-permute-start(bf16[1024,384]{1,0:T(8,128)(2,1)} %bitcast.30), channel_id=1, source_target_pairs={{0,4},{4,8},{8,12},{12,14},{14,10},{10,6},{6,2},{2,0},{1,5},{5,9},... | collective-permute-start | bytes 2359304 | tf_op jit(solution)/shard_map/ppermute | solution.py:62
  3.7 19.3 %collective-permute-start.1 = (bf16[1024,384]{1,0:T(8,128)(2,1)}, bf16[1024,384]{1,0:T(8,128)(2,1)}, u32[]{:S(2)}, u32[]{:S(2)}) collective-permute-start(bf16[1024,384]{1,0:T(8,128)(2,1)} %bitcast.31), channel_id=1, source_target_pairs={{4,0},{8,4},{12,8},{14,12},{10,14},{6,10},{2,6},{0,2},{5,1},{9,5},... | collective-permute-start | bytes 2359304 | tf_op jit(solution)/shard_map/ppermute | solution.py:62
  9.5 19.1 %copy-start.1 = (f32[512,384]{0,1:T(8,128)S(1)}, f32[512,384]{0,1:T(8,128)}, u32[]{:S(2)}) copy-start(f32[512,384]{0,1:T(8,128)} %convolution_bitcast_fusion) | copy-start | bytes 2359300
  24.1 9.7 %collective-permute-start.2 = (bf16[512,384]{1,0:T(8,128)(2,1)S(1)}, bf16[512,384]{1,0:T(8,128)(2,1)S(1)}, u32[]{:S(2)}, u32[]{:S(2)}) collective-permute-start(bf16[512,384]{1,0:T(8,128)(2,1)S(1)} %slice.128), channel_id=1, source_target_pairs={{0,4},{4,8},{8,12},{12,14},{14,10},{10,6},{6,2},{2,0},{1,5},{5,9},... | collective-permute-start | bytes 1179656 | tf_op jit(solution)/shard_map/ppermute | solution.py:62
  26.8 9.4 %collective-permute-start.3 = (bf16[512,384]{1,0:T(8,128)(2,1)S(1)}, bf16[512,384]{1,0:T(8,128)(2,1)S(1)}, u32[]{:S(2)}, u32[]{:S(2)}) collective-permute-start(bf16[512,384]{1,0:T(8,128)(2,1)S(1)} %slice.129), channel_id=1, source_target_pairs={{4,0},{8,4},{12,8},{14,12},{10,14},{6,10},{2,6},{0,2},{5,1},{9,5},... | collective-permute-start | bytes 1179656 | tf_op jit(solution)/shard_map/ppermute | solution.py:62
  36.2 8.5 %collective-permute-start.4 = (bf16[512,384]{1,0:T(8,128)(2,1)S(1)}, bf16[512,384]{1,0:T(8,128)(2,1)S(1)}, u32[]{:S(2)}, u32[]{:S(2)}) collective-permute-start(bf16[512,384]{1,0:T(8,128)(2,1)S(1)} %collective-permute-done.2), channel_id=1, source_target_pairs={{0,4},{4,8},{8,12},{12,14},{14,10},{10,6},{6,2},{2,0},{1,5},{5,9},... | collective-permute-start | bytes 1179656 | tf_op jit(solution)/shard_map/ppermute | solution.py:62
  37.8 9.3 %collective-permute-start.5 = (bf16[512,384]{1,0:T(8,128)(2,1)S(1)}, bf16[512,384]{1,0:T(8,128)(2,1)S(1)}, u32[]{:S(2)}, u32[]{:S(2)}) collective-permute-start(bf16[512,384]{1,0:T(8,128)(2,1)S(1)} %collective-permute-done.3), channel_id=1, source_target_pairs={{4,0},{8,4},{12,8},{14,12},{10,14},{6,10},{2,6},{0,2},{5,1},{9,5},... | collective-permute-start | bytes 1179656 | tf_op jit(solution)/shard_map/ppermute | solution.py:62
  47.1 11.8 %collective-permute-start.9 = (bf16[512,384]{1,0:T(8,128)(2,1)S(1)}, bf16[512,384]{1,0:T(8,128)(2,1)S(1)}, u32[]{:S(2)}, u32[]{:S(2)}) collective-permute-start(bf16[512,384]{1,0:T(8,128)(2,1)S(1)} %collective-permute-done.5), channel_id=1, source_target_pairs={{4,0},{8,4},{12,8},{14,12},{10,14},{6,10},{2,6},{0,2},{5,1},{9,5},... | collective-permute-start | bytes 1179656 | tf_op jit(solution)/shard_map/ppermute | solution.py:62
  48.6 10.2 %collective-permute-start.8 = (bf16[512,384]{1,0:T(8,128)(2,1)S(1)}, bf16[512,384]{1,0:T(8,128)(2,1)S(1)}, u32[]{:S(2)}, u32[]{:S(2)}) collective-permute-start(bf16[512,384]{1,0:T(8,128)(2,1)S(1)} %collective-permute-done.4), channel_id=1, source_target_pairs={{0,4},{4,8},{8,12},{12,14},{14,10},{10,6},{6,2},{2,0},{1,5},{5,9},... | collective-permute-start | bytes 1179656 | tf_op jit(solution)/shard_map/ppermute | solution.py:62
  51.8 14.1 %collective-permute-start.6 = (bf16[512,384]{1,0:T(8,128)(2,1)S(1)}, bf16[512,384]{1,0:T(8,128)(2,1)S(1)}, u32[]{:S(2)}, u32[]{:S(2)}) collective-permute-start(bf16[512,384]{1,0:T(8,128)(2,1)S(1)} %slice.130), channel_id=1, source_target_pairs={{4,0},{8,4},{12,8},{14,12},{10,14},{6,10},{2,6},{0,2},{5,1},{9,5},... | collective-permute-start | bytes 1179656 | tf_op jit(solution)/shard_map/ppermute | solution.py:62
  52.3 13.6 %collective-permute-start.7 = (bf16[512,384]{1,0:T(8,128)(2,1)S(1)}, bf16[512,384]{1,0:T(8,128)(2,1)S(1)}, u32[]{:S(2)}, u32[]{:S(2)}) collective-permute-start(bf16[512,384]{1,0:T(8,128)(2,1)S(1)} %slice.131), channel_id=1, source_target_pairs={{0,4},{4,8},{8,12},{12,14},{14,10},{10,6},{6,2},{2,0},{1,5},{5,9},... | collective-permute-start | bytes 1179656 | tf_op jit(solution)/shard_map/ppermute | solution.py:62
  61.6 6.9 %collective-permute-start.14 = (f32[8,8]{1,0:T(8,128)S(1)}, f32[8,8]{1,0:T(8,128)S(1)}, u32[]{:S(2)}, u32[]{:S(2)}) collective-permute-start(f32[8,8]{1,0:T(8,128)S(1)} %fusion.93), channel_id=1, source_target_pairs={{0,6},{2,4},{4,2},{6,0},{8,14},{10,12},{12,10},{14,8},{1,7},{3,5},... | collective-permute-start | bytes 776 | tf_op jit(solution)/shard_map/ppermute | solution.py:95
  62.7 5.8 %collective-permute-start.13 = (f32[8,8]{1,0:T(8,128)S(1)}, f32[8,8]{1,0:T(8,128)S(1)}, u32[]{:S(2)}, u32[]{:S(2)}) collective-permute-start(f32[8,8]{1,0:T(8,128)S(1)} %fusion.93), channel_id=1, source_target_pairs={{0,4},{2,6},{4,0},{6,2},{8,12},{10,14},{12,8},{14,10},{1,5},{3,7},... | collective-permute-start | bytes 776 | tf_op jit(solution)/shard_map/ppermute | solution.py:95
  63.5 5.0 %collective-permute-start.12 = (f32[8,8]{1,0:T(8,128)S(1)}, f32[8,8]{1,0:T(8,128)S(1)}, u32[]{:S(2)}, u32[]{:S(2)}) collective-permute-start(f32[8,8]{1,0:T(8,128)S(1)} %fusion.93), channel_id=1, source_target_pairs={{0,2},{2,0},{4,6},{6,4},{8,10},{10,8},{12,14},{14,12},{1,3},{3,1},... | collective-permute-start | bytes 776 | tf_op jit(solution)/shard_map/ppermute | solution.py:95
  66.0 8.9 %collective-permute-start.10 = (bf16[512,384]{1,0:T(8,128)(2,1)S(1)}, bf16[512,384]{1,0:T(8,128)(2,1)S(1)}, u32[]{:S(2)}, u32[]{:S(2)}) collective-permute-start(bf16[512,384]{1,0:T(8,128)(2,1)S(1)} %collective-permute-done.6), channel_id=1, source_target_pairs={{4,0},{8,4},{12,8},{14,12},{10,14},{6,10},{2,6},{0,2},{5,1},{9,5},... | collective-permute-start | bytes 1179656 | tf_op jit(solution)/shard_map/ppermute | solution.py:62
  66.9 8.0 %collective-permute-start.11 = (bf16[512,384]{1,0:T(8,128)(2,1)S(1)}, bf16[512,384]{1,0:T(8,128)(2,1)S(1)}, u32[]{:S(2)}, u32[]{:S(2)}) collective-permute-start(bf16[512,384]{1,0:T(8,128)(2,1)S(1)} %collective-permute-done.7), channel_id=1, source_target_pairs={{0,4},{4,8},{8,12},{12,14},{14,10},{10,6},{6,2},{2,0},{1,5},{5,9},... | collective-permute-start | bytes 1179656 | tf_op jit(solution)/shard_map/ppermute | solution.py:62
  68.5 6.3 %collective-permute-start.15 = (f32[8,8]{1,0:T(8,128)S(1)}, f32[8,8]{1,0:T(8,128)S(1)}, u32[]{:S(2)}, u32[]{:S(2)}) collective-permute-start(f32[8,8]{1,0:T(8,128)S(1)} %add_add_fusion.2), channel_id=1, source_target_pairs={{0,8},{2,10},{4,12},{6,14},{8,0},{10,2},{12,4},{14,6},{1,9},{3,11}... | collective-permute-start | bytes 776 | tf_op jit(solution)/shard_map/ppermute | solution.py:95
  75.7 1.7 %collective-permute-start.16 = (f32[8,8]{1,0:T(8,128)S(1)}, f32[8,8]{1,0:T(8,128)S(1)}, u32[]{:S(2)}, u32[]{:S(2)}) collective-permute-start(f32[8,8]{1,0:T(8,128)S(1)} %add.279), channel_id=1, source_target_pairs={{0,1},{1,0},{2,3},{3,2},{4,5},{5,4},{6,7},{7,6},{8,9},{9,8},{10,11... | collective-permute-start | bytes 776 | tf_op jit(solution)/shard_map/ppermute | solution.py:95

commit v5 on v4

--- a/solution.py
+++ b/solution.py
@@ -68,7 +68,7 @@
     opposite = lax.dynamic_slice(weights_slab, (0, starts[half]), (depth, depth))
     across = lax.dot_general(weighted, opposite, (((1,), (0,)), ((), ())), preferred_element_type=jnp.float32)
     across = two_terms(0.5 * across)
-    came_forth, came_back, own, weighted, across = together((came_forth, came_back, own, weighted, across))
+    came_forth, came_back, across = together((came_forth, came_back, across))
 
     block, came, late = [came_forth[upper], came_back[lower]], (came_back, came_forth), None
     near = [0.5 * own[0] + product(block[0], -1), 0.5 * own[1] + product(block[1], 1)]
@@ -109,7 +109,6 @@
     rest = [near[h] + rest[h] for h in (0, 1)]
     far = [product(far[h], half) for h in (0, 1)]
     rest = [rest[h] + far[h] for h in (0, 1)]
-    late, rest = together((late, rest))
     rest = [rest[0] + product(late[0], half - 2), rest[1] + product(late[1], 2 - half)]
     late = move(late, (back, forth))
     share = exchange(share, 2)

time: 78.7 us -> 78 us (level)
    convert_element_type x0 -> x1, other arithmetic: none -> 1.34 us  [local(): (pairs.astype(jnp.float32) * coeff[:, None, None]).astype(jnp.bfloat16)]
    reshape x1 -> x0, other arithmetic: 1.34 us -> none  [local(): (pairs.astype(jnp.float32) * coeff[:, None, None]).astype(jnp.bfloat16)]
  transfers between devices with their start and end apart: 17 -> 17, of which waited for: 8 -> 9; matrix products, arithmetic and copies ran while one was open for 32% -> 31% of each run, Pallas kernels for 0% -> 0%
where the time goes in v5:
time: 78 us; the launch traced here: 77.4 us
  waiting for transfers between devices  29.7 us (38%)
  starting transfers between devices  19.6 us (25%)
  matrix products  18.5 us (24%)
  local copies, waits for them, and re-layouts  5.4 us (7%)
  other arithmetic  2.98 us (4%)
  between operations  1.25 us (2%)
    ppermute x12, waiting for transfers between devices, move(): return [lax.ppermute(block, 'blk', way) for block, way in zip(pair, ways)]  27.2 us
    dot_general x32, matrix products, times(): lax.dot_general(left, right, (((1,), (1,)), ((), ())), preferred_element_...  17.2 us
    ppermute x12, starting transfers between devices, move(): return [lax.ppermute(block, 'blk', way) for block, way in zip(pair, ways)]  13.5 us
    ppermute x5, starting transfers between devices, exchange(): lax.ppermute(share, axis, [(i, i ^ k) for i in range(size)])  6.08 us
    ppermute x5, waiting for transfers between devices, exchange(): lax.ppermute(share, axis, [(i, i ^ k) for i in range(size)])  2.53 us
    slice x2, local copies, waits for them, and re-layouts, local(): late = [came[0][upper], came[1][lower]]  2.07 us
  transfers between devices with their start and end apart: 17, of which 9 were waited for; matrix products, arithmetic and copies ran while one was open for 31% of the time, Pallas kernels for 0%

profile of v5, /device:TPU:0, one launch (start us, length us, event | category | flops | bytes accessed | tf_op | source)
XLA Modules:
  0.0 77.4 jit_solution(10180203135041172363)
XLA Ops:
  0.7 3.1 %collective-permute-start = (bf16[1024,384]{1,0:T(8,128)(2,1)}, bf16[1024,384]{1,0:T(8,128)(2,1)}, u32[]{:S(2)}, u32[]{:S(2)}) collective-permute-start(bf16[1024,384]{1,0:T(8,128)(2,1)} %bitcast.48), channel_id=1, source_target_pairs={{0,4},{4,8},{8,12},{12,14},{14,10},{10,6},{6,2},{2,0},{1,5},{5,9},... | collective-permute-start | bytes 2359304 | tf_op jit(solution)/shard_map/ppermute | solution.py:62
  3.7 2.3 %fusion.2 = f32[512,384]{0,1:T(8,128)} fusion(bf16[128,8,384]{2,1,0:T(8,128)(2,1)} %param.4, bf16[384,3072]{1,0:T(8,128)(2,1)S(1)} %copy-done, s32[]{:T(128)S(6)} %select_n.142), kind=kOutput, calls=%fused_computation.10 | convolution fusion | flops 151191552 | bytes 1474564 | tf_op jit(solution)/shard_map/dot_general | solution.py:23
  6.1 1.4 %fusion.1 = f32[512,384]{0,1:T(8,128)S(1)} fusion(bf16[128,8,384]{2,1,0:T(8,128)(2,1)} %param.4, bf16[384,3072]{1,0:T(8,128)(2,1)S(1)} %copy-done, s32[]{:T(128)S(6)} %select_n.142), kind=kOutput, calls=%fused_computation.7 | convolution fusion | flops 151191552 | bytes 1474564 | tf_op jit(solution)/shard_map/dot_general | solution.py:23
  7.7 1.3 %multiply_convert_fusion = bf16[128,8,384]{2,1,0:T(8,128)(2,1)S(1)} fusion(bf16[128,8,384]{2,1,0:T(8,128)(2,1)} %param.4, f32[128]{0:T(128)S(1)} %convert_subtract_fusion), kind=kLoop, calls=%fused_computation.3 | loop fusion | flops 1179648 | bytes 1573376 | tf_op jit(solution)/shard_map/convert_element_type | solution.py:67
  9.7 11.8 %collective-permute-done = bf16[1024,384]{1,0:T(8,128)(2,1)} collective-permute-done((bf16[1024,384]{1,0:T(8,128)(2,1)}, bf16[1024,384]{1,0:T(8,128)(2,1)}, u32[]{:S(2)}, u32[]{:S(2)}) %collective-permute-start) | collective-permute-done | bytes 786464 | tf_op jit(solution)/shard_map/ppermute | solution.py:62
  21.5 1.5 %collective-permute-done.1 = bf16[1024,384]{1,0:T(8,128)(2,1)} collective-permute-done((bf16[1024,384]{1,0:T(8,128)(2,1)}, bf16[1024,384]{1,0:T(8,128)(2,1)}, u32[]{:S(2)}, u32[]{:S(2)}) %collective-permute-start.1) | collective-permute-done | bytes 786464 | tf_op jit(solution)/shard_map/ppermute | solution.py:62
  24.1 1.6 %collective-permute-start.2 = (bf16[512,384]{1,0:T(8,128)(2,1)S(1)}, bf16[512,384]{1,0:T(8,128)(2,1)S(1)}, u32[]{:S(2)}, u32[]{:S(2)}) collective-permute-start(bf16[512,384]{1,0:T(8,128)(2,1)S(1)} %slice.138), channel_id=1, source_target_pairs={{0,4},{4,8},{8,12},{12,14},{14,10},{10,6},{6,2},{2,0},{1,5},{5,9},... | collective-permute-start | bytes 1179656 | tf_op jit(solution)/shard_map/ppermute | solution.py:62
  27.3 1.4 %convolution_add_fusion.1 = f32[512,384]{0,1:T(8,128)S(1)} fusion(f32[512,384]{0,1:T(8,128)S(1)} %copy-done.1, bf16[384,3072]{1,0:T(8,128)(2,1)S(1)} %copy-done, s32[]{:T(128)S(6)} %select_n.145, bf16[1024,384]{1,0:T(8,128)(2,1)} %collective-permute-done), kind=kOutput, calls=%fused_computation.8 | convolution fusion | flops 151191552 | bytes 2260996 | tf_op jit(solution)/shard_map/dot_general | solution.py:23
  28.7 1.4 %convolution_add_fusion = f32[512,384]{0,1:T(8,128)S(1)} fusion(f32[512,384]{0,1:T(8,128)S(1)} %fusion.1, bf16[384,3072]{1,0:T(8,128)(2,1)S(1)} %copy-done, s32[]{:T(128)S(6)} %select_n.148, bf16[1024,384]{1,0:T(8,128)(2,1)} %collective-permute-done.1), kind=kOutput, calls=%fused_computation.5 | convolution fusion | flops 151191552 | bytes 2260996 | tf_op jit(solution)/shard_map/dot_general | solution.py:23
  30.1 3.7 %collective-permute-done.2 = bf16[512,384]{1,0:T(8,128)(2,1)S(1)} collective-permute-done((bf16[512,384]{1,0:T(8,128)(2,1)S(1)}, bf16[512,384]{1,0:T(8,128)(2,1)S(1)}, u32[]{:S(2)}, u32[]{:S(2)}) %collective-permute-start.2) | collective-permute-done | bytes 393248 | tf_op jit(solution)/shard_map/ppermute | solution.py:62
  33.8 2.4 %collective-permute-done.3 = bf16[512,384]{1,0:T(8,128)(2,1)S(1)} collective-permute-done((bf16[512,384]{1,0:T(8,128)(2,1)S(1)}, bf16[512,384]{1,0:T(8,128)(2,1)S(1)}, u32[]{:S(2)}, u32[]{:S(2)}) %collective-permute-start.3) | collective-permute-done | bytes 393248 | tf_op jit(solution)/shard_map/ppermute | solution.py:62
  36.2 1.6 %collective-permute-start.4 = (bf16[512,384]{1,0:T(8,128)(2,1)S(1)}, bf16[512,384]{1,0:T(8,128)(2,1)S(1)}, u32[]{:S(2)}, u32[]{:S(2)}) collective-permute-start(bf16[512,384]{1,0:T(8,128)(2,1)S(1)} %collective-permute-done.2), channel_id=1, source_target_pairs={{0,4},{4,8},{8,12},{12,14},{14,10},{10,6},{6,2},{2,0},{1,5},{5,9},... | collective-permute-start | bytes 1179656 | tf_op jit(solution)/shard_map/ppermute | solution.py:62
  41.4 1.4 %fusion.40 = f32[512,384]{0,1:T(8,128)S(1)} fusion(bf16[384,3072]{1,0:T(8,128)(2,1)S(1)} %copy-done, s32[]{:T(128)S(6)} %select_n.148, bf16[1024,384]{1,0:T(8,128)(2,1)} %collective-permute-done.1), kind=kOutput, calls=%fused_computation.61 | convolution fusion | flops 150994944 | bytes 1474564 | tf_op jit(solution)/shard_map/dot_general | solution.py:23
  43.0 1.4 %fusion.43 = f32[512,384]{0,1:T(8,128)S(1)} fusion(bf16[384,3072]{1,0:T(8,128)(2,1)S(1)} %copy-done, s32[]{:T(128)S(6)} %select_n.145, bf16[1024,384]{1,0:T(8,128)(2,1)} %collective-permute-done), kind=kOutput, calls=%fused_computation.64 | convolution fusion | flops 150994944 | bytes 1474564 | tf_op jit(solution)/shard_map/dot_general | solution.py:23
  44.7 2.4 %collective-permute-done.5 = bf16[512,384]{1,0:T(8,128)(2,1)S(1)} collective-permute-done((bf16[512,384]{1,0:T(8,128)(2,1)S(1)}, bf16[512,384]{1,0:T(8,128)(2,1)S(1)}, u32[]{:S(2)}, u32[]{:S(2)}) %collective-permute-start.5) | collective-permute-done | bytes 393248 | tf_op jit(solution)/shard_map/ppermute | solution.py:62
  48.6 1.6 %collective-permute-start.10 = (bf16[512,384]{1,0:T(8,128)(2,1)S(1)}, bf16[512,384]{1,0:T(8,128)(2,1)S(1)}, u32[]{:S(2)}, u32[]{:S(2)}) collective-permute-start(bf16[512,384]{1,0:T(8,128)(2,1)S(1)} %collective-permute-done.4), channel_id=1, source_target_pairs={{0,4},{4,8},{8,12},{12,14},{14,10},{10,6},{6,2},{2,0},{1,5},{5,9},... | collective-permute-start | bytes 1179656 | tf_op jit(solution)/shard_map/ppermute | solution.py:62
  52.3 1.6 %collective-permute-start.8 = (bf16[512,384]{1,0:T(8,128)(2,1)S(1)}, bf16[512,384]{1,0:T(8,128)(2,1)S(1)}, u32[]{:S(2)}, u32[]{:S(2)}) collective-permute-start(bf16[512,384]{1,0:T(8,128)(2,1)S(1)} %slice.145), channel_id=1, source_target_pairs={{0,4},{4,8},{8,12},{12,14},{14,10},{10,6},{6,2},{2,0},{1,5},{5,9},... | collective-permute-start | bytes 1179656 | tf_op jit(solution)/shard_map/ppermute | solution.py:62
  53.9 4.9 %collective-permute-done.10 = bf16[512,384]{1,0:T(8,128)(2,1)S(1)} collective-permute-done((bf16[512,384]{1,0:T(8,128)(2,1)S(1)}, bf16[512,384]{1,0:T(8,128)(2,1)S(1)}, u32[]{:S(2)}, u32[]{:S(2)}) %collective-permute-start.10) | collective-permute-done | bytes 393248 | tf_op jit(solution)/shard_map/ppermute | solution.py:62
  61.6 1.1 %collective-permute-start.14 = (f32[8,8]{1,0:T(8,128)S(1)}, f32[8,8]{1,0:T(8,128)S(1)}, u32[]{:S(2)}, u32[]{:S(2)}) collective-permute-start(f32[8,8]{1,0:T(8,128)S(1)} %fusion.87), channel_id=1, source_target_pairs={{0,6},{2,4},{4,2},{6,0},{8,14},{10,12},{12,10},{14,8},{1,7},{3,5},... | collective-permute-start | bytes 776 | tf_op jit(solution)/shard_map/ppermute | solution.py:95
  63.5 1.6 %collective-permute-start.12 = (f32[8,8]{1,0:T(8,128)S(1)}, f32[8,8]{1,0:T(8,128)S(1)}, u32[]{:S(2)}, u32[]{:S(2)}) collective-permute-start(f32[8,8]{1,0:T(8,128)S(1)} %fusion.87), channel_id=1, source_target_pairs={{0,2},{2,0},{4,6},{6,4},{8,10},{10,8},{12,14},{14,12},{1,3},{3,1},... | collective-permute-start | bytes 776 | tf_op jit(solution)/shard_map/ppermute | solution.py:95
  66.4 1.6 %collective-permute-start.9 = (bf16[512,384]{1,0:T(8,128)(2,1)S(1)}, bf16[512,384]{1,0:T(8,128)(2,1)S(1)}, u32[]{:S(2)}, u32[]{:S(2)}) collective-permute-start(bf16[512,384]{1,0:T(8,128)(2,1)S(1)} %collective-permute-done.8), channel_id=1, source_target_pairs={{0,4},{4,8},{8,12},{12,14},{14,10},{10,6},{6,2},{2,0},{1,5},{5,9},... | collective-permute-start | bytes 1179656 | tf_op jit(solution)/shard_map/ppermute | solution.py:62
  68.5 2.5 %collective-permute-start.15 = (f32[8,8]{1,0:T(8,128)S(1)}, f32[8,8]{1,0:T(8,128)S(1)}, u32[]{:S(2)}, u32[]{:S(2)}) collective-permute-start(f32[8,8]{1,0:T(8,128)S(1)} %add_add_fusion.2), channel_id=1, source_target_pairs={{0,8},{2,10},{4,12},{6,14},{8,0},{10,2},{12,4},{14,6},{1,9},{3,11}... | collective-permute-start | bytes 776 | tf_op jit(solution)/shard_map/ppermute | solution.py:95
  71.4 2.5 %collective-permute-done.15 = f32[8,8]{1,0:T(8,128)S(1)} collective-permute-done((f32[8,8]{1,0:T(8,128)S(1)}, f32[8,8]{1,0:T(8,128)S(1)}, u32[]{:S(2)}, u32[]{:S(2)}) %collective-permute-start.15) | collective-permute-done | bytes 288 | tf_op jit(solution)/shard_map/ppermute | solution.py:95
  75.6 1.2 %copy.35 = bf16[1024,384]{1,0:T(8,128)(2,1)} copy(bf16[1024,384]{0,1:T(8,128)(2,1)S(1)} %pad_maximum_fusion) | data formatting | bytes 1572864 | tf_op jit(solution)/shard_map/concatenate | solution.py:119
  (71 shorter events, 18.8 us)
Async XLA Ops:
  0.6 3.1 %copy-start = (bf16[384,3072]{1,0:T(8,128)(2,1)S(1)}, bf16[384,3072]{1,0:T(8,128)(2,1)}, u32[]{:S(2)}) copy-start(bf16[384,3072]{1,0:T(8,128)(2,1)} %param.3) | copy-start | bytes 7077892
  0.6 7.0 %copy-start.2 = (s32[128]{0:T(128)S(1)}, s32[128]{0:T(128)}, u32[]{:S(2)}) copy-start(s32[128]{0:T(128)} %param.5) | copy-start | bytes 1540
  0.7 20.9 %collective-permute-start = (bf16[1024,384]{1,0:T(8,128)(2,1)}, bf16[1024,384]{1,0:T(8,128)(2,1)}, u32[]{:S(2)}, u32[]{:S(2)}) collective-permute-start(bf16[1024,384]{1,0:T(8,128)(2,1)} %bitcast.48), channel_id=1, source_target_pairs={{0,4},{4,8},{8,12},{12,14},{14,10},{10,6},{6,2},{2,0},{1,5},{5,9},... | collective-permute-start | bytes 2359304 | tf_op jit(solution)/shard_map/ppermute | solution.py:62
  3.7 19.3 %collective-permute-start.1 = (bf16[1024,384]{1,0:T(8,128)(2,1)}, bf16[1024,384]{1,0:T(8,128)(2,1)}, u32[]{:S(2)}, u32[]{:S(2)}) collective-permute-start(bf16[1024,384]{1,0:T(8,128)(2,1)} %bitcast.49), channel_id=1, source_target_pairs={{4,0},{8,4},{12,8},{14,12},{10,14},{6,10},{2,6},{0,2},{5,1},{9,5},... | collective-permute-start | bytes 2359304 | tf_op jit(solution)/shard_map/ppermute | solution.py:62
  9.0 18.2 %copy-start.1 = (f32[512,384]{0,1:T(8,128)S(1)}, f32[512,384]{0,1:T(8,128)}, u32[]{:S(2)}) copy-start(f32[512,384]{0,1:T(8,128)} %fusion.2) | copy-start | bytes 2359300
  24.1 9.7 %collective-permute-start.2 = (bf16[512,384]{1,0:T(8,128)(2,1)S(1)}, bf16[512,384]{1,0:T(8,128)(2,1)S(1)}, u32[]{:S(2)}, u32[]{:S(2)}) collective-permute-start(bf16[512,384]{1,0:T(8,128)(2,1)S(1)} %slice.138), channel_id=1, source_target_pairs={{0,4},{4,8},{8,12},{12,14},{14,10},{10,6},{6,2},{2,0},{1,5},{5,9},... | collective-permute-start | bytes 1179656 | tf_op jit(solution)/shard_map/ppermute | solution.py:62
  26.8 9.4 %collective-permute-start.3 = (bf16[512,384]{1,0:T(8,128)(2,1)S(1)}, bf16[512,384]{1,0:T(8,128)(2,1)S(1)}, u32[]{:S(2)}, u32[]{:S(2)}) collective-permute-start(bf16[512,384]{1,0:T(8,128)(2,1)S(1)} %slice.139), channel_id=1, source_target_pairs={{4,0},{8,4},{12,8},{14,12},{10,14},{6,10},{2,6},{0,2},{5,1},{9,5},... | collective-permute-start | bytes 1179656 | tf_op jit(solution)/shard_map/ppermute | solution.py:62
  36.2 8.5 %collective-permute-start.4 = (bf16[512,384]{1,0:T(8,128)(2,1)S(1)}, bf16[512,384]{1,0:T(8,128)(2,1)S(1)}, u32[]{:S(2)}, u32[]{:S(2)}) collective-permute-start(bf16[512,384]{1,0:T(8,128)(2,1)S(1)} %collective-permute-done.2), channel_id=1, source_target_pairs={{0,4},{4,8},{8,12},{12,14},{14,10},{10,6},{6,2},{2,0},{1,5},{5,9},... | collective-permute-start | bytes 1179656 | tf_op jit(solution)/shard_map/ppermute | solution.py:62
  37.8 9.3 %collective-permute-start.5 = (bf16[512,384]{1,0:T(8,128)(2,1)S(1)}, bf16[512,384]{1,0:T(8,128)(2,1)S(1)}, u32[]{:S(2)}, u32[]{:S(2)}) collective-permute-start(bf16[512,384]{1,0:T(8,128)(2,1)S(1)} %collective-permute-done.3), channel_id=1, source_target_pairs={{4,0},{8,4},{12,8},{14,12},{10,14},{6,10},{2,6},{0,2},{5,1},{9,5},... | collective-permute-start | bytes 1179656 | tf_op jit(solution)/shard_map/ppermute | solution.py:62
  47.1 11.8 %collective-permute-start.11 = (bf16[512,384]{1,0:T(8,128)(2,1)S(1)}, bf16[512,384]{1,0:T(8,128)(2,1)S(1)}, u32[]{:S(2)}, u32[]{:S(2)}) collective-permute-start(bf16[512,384]{1,0:T(8,128)(2,1)S(1)} %collective-permute-done.5), channel_id=1, source_target_pairs={{4,0},{8,4},{12,8},{14,12},{10,14},{6,10},{2,6},{0,2},{5,1},{9,5},... | collective-permute-start | bytes 1179656 | tf_op jit(solution)/shard_map/ppermute | solution.py:62
  48.6 10.2 %collective-permute-start.10 = (bf16[512,384]{1,0:T(8,128)(2,1)S(1)}, bf16[512,384]{1,0:T(8,128)(2,1)S(1)}, u32[]{:S(2)}, u32[]{:S(2)}) collective-permute-start(bf16[512,384]{1,0:T(8,128)(2,1)S(1)} %collective-permute-done.4), channel_id=1, source_target_pairs={{0,4},{4,8},{8,12},{12,14},{14,10},{10,6},{6,2},{2,0},{1,5},{5,9},... | collective-permute-start | bytes 1179656 | tf_op jit(solution)/shard_map/ppermute | solution.py:62
  51.8 13.3 %collective-permute-start.6 = (bf16[512,384]{1,0:T(8,128)(2,1)S(1)}, bf16[512,384]{1,0:T(8,128)(2,1)S(1)}, u32[]{:S(2)}, u32[]{:S(2)}) collective-permute-start(bf16[512,384]{1,0:T(8,128)(2,1)S(1)} %slice.144), channel_id=1, source_target_pairs={{4,0},{8,4},{12,8},{14,12},{10,14},{6,10},{2,6},{0,2},{5,1},{9,5},... | collective-permute-start | bytes 1179656 | tf_op jit(solution)/shard_map/ppermute | solution.py:62
  52.3 14.0 %collective-permute-start.8 = (bf16[512,384]{1,0:T(8,128)(2,1)S(1)}, bf16[512,384]{1,0:T(8,128)(2,1)S(1)}, u32[]{:S(2)}, u32[]{:S(2)}) collective-permute-start(bf16[512,384]{1,0:T(8,128)(2,1)S(1)} %slice.145), channel_id=1, source_target_pairs={{0,4},{4,8},{8,12},{12,14},{14,10},{10,6},{6,2},{2,0},{1,5},{5,9},... | collective-permute-start | bytes 1179656 | tf_op jit(solution)/shard_map/ppermute | solution.py:62
  61.6 6.8 %collective-permute-start.14 = (f32[8,8]{1,0:T(8,128)S(1)}, f32[8,8]{1,0:T(8,128)S(1)}, u32[]{:S(2)}, u32[]{:S(2)}) collective-permute-start(f32[8,8]{1,0:T(8,128)S(1)} %fusion.87), channel_id=1, source_target_pairs={{0,6},{2,4},{4,2},{6,0},{8,14},{10,12},{12,10},{14,8},{1,7},{3,5},... | collective-permute-start | bytes 776 | tf_op jit(solution)/shard_map/ppermute | solution.py:95
  62.7 5.8 %collective-permute-start.13 = (f32[8,8]{1,0:T(8,128)S(1)}, f32[8,8]{1,0:T(8,128)S(1)}, u32[]{:S(2)}, u32[]{:S(2)}) collective-permute-start(f32[8,8]{1,0:T(8,128)S(1)} %fusion.87), channel_id=1, source_target_pairs={{0,4},{2,6},{4,0},{6,2},{8,12},{10,14},{12,8},{14,10},{1,5},{3,7},... | collective-permute-start | bytes 776 | tf_op jit(solution)/shard_map/ppermute | solution.py:95
  63.5 4.9 %collective-permute-start.12 = (f32[8,8]{1,0:T(8,128)S(1)}, f32[8,8]{1,0:T(8,128)S(1)}, u32[]{:S(2)}, u32[]{:S(2)}) collective-permute-start(f32[8,8]{1,0:T(8,128)S(1)} %fusion.87), channel_id=1, source_target_pairs={{0,2},{2,0},{4,6},{6,4},{8,10},{10,8},{12,14},{14,12},{1,3},{3,1},... | collective-permute-start | bytes 776 | tf_op jit(solution)/shard_map/ppermute | solution.py:95
  65.1 8.8 %collective-permute-start.7 = (bf16[512,384]{1,0:T(8,128)(2,1)S(1)}, bf16[512,384]{1,0:T(8,128)(2,1)S(1)}, u32[]{:S(2)}, u32[]{:S(2)}) collective-permute-start(bf16[512,384]{1,0:T(8,128)(2,1)S(1)} %collective-permute-done.6), channel_id=1, source_target_pairs={{4,0},{8,4},{12,8},{14,12},{10,14},{6,10},{2,6},{0,2},{5,1},{9,5},... | collective-permute-start | bytes 1179656 | tf_op jit(solution)/shard_map/ppermute | solution.py:62
  66.4 7.8 %collective-permute-start.9 = (bf16[512,384]{1,0:T(8,128)(2,1)S(1)}, bf16[512,384]{1,0:T(8,128)(2,1)S(1)}, u32[]{:S(2)}, u32[]{:S(2)}) collective-permute-start(bf16[512,384]{1,0:T(8,128)(2,1)S(1)} %collective-permute-done.8), channel_id=1, source_target_pairs={{0,4},{4,8},{8,12},{12,14},{14,10},{10,6},{6,2},{2,0},{1,5},{5,9},... | collective-permute-start | bytes 1179656 | tf_op jit(solution)/shard_map/ppermute | solution.py:62
  68.5 5.5 %collective-permute-start.15 = (f32[8,8]{1,0:T(8,128)S(1)}, f32[8,8]{1,0:T(8,128)S(1)}, u32[]{:S(2)}, u32[]{:S(2)}) collective-permute-start(f32[8,8]{1,0:T(8,128)S(1)} %add_add_fusion.2), channel_id=1, source_target_pairs={{0,8},{2,10},{4,12},{6,14},{8,0},{10,2},{12,4},{14,6},{1,9},{3,11}... | collective-permute-start | bytes 776 | tf_op jit(solution)/shard_map/ppermute | solution.py:95
  75.0 1.7 %collective-permute-start.16 = (f32[8,8]{1,0:T(8,128)S(1)}, f32[8,8]{1,0:T(8,128)S(1)}, u32[]{:S(2)}, u32[]{:S(2)}) collective-permute-start(f32[8,8]{1,0:T(8,128)S(1)} %add.275), channel_id=1, source_target_pairs={{0,1},{1,0},{2,3},{3,2},{4,5},{5,4},{6,7},{7,6},{8,9},{9,8},{10,11... | collective-permute-start | bytes 776 | tf_op jit(solution)/shard_map/ppermute | solution.py:95
